TPU v7x, 512 devices: a whole 4x8x8 slice. The times are simulated.
512 devices in a mesh: row: 32 (over x, z_lo, core), ch: 16 (over y, z_hi).
Axes of the slice: x: 4, y: 8, z: 8 (z_hi: 2, z_lo: 4; z = z_hi * 4 + z_lo), core: 2. Of those that a mesh axis runs over, the one named last changes fastest.
Arguments:
- pair: float32 [512, 512, 128], P('row', 'ch'), may hold values from -6 to 6
- out_inputs: bfloat16 [128, 512], replicated, may hold values from -0.5 to 0.5
- out_gate: bfloat16 [128, 128], replicated, may hold values from -0.5 to 0.5
- out_final: bfloat16 [128, 128], replicated, may hold values from -0.5 to 0.5
- in_inputs: bfloat16 [128, 512], replicated, may hold values from -0.5 to 0.5
- in_gate: bfloat16 [128, 128], replicated, may hold values from -0.5 to 0.5
- in_final: bfloat16 [128, 128], replicated, may hold values from -0.5 to 0.5
Outputs:
- updated: float32 [512, 512, 128], P('row', 'ch')
All inputs are finite; a program needn't handle non-finite values.
Results may differ from a plain program's by a relative error of at most 0.0065.
Values may be sent and summed in bfloat16 or wider, within the bound.
A program may use at most 64 MiB of HBM per device.

v0:
```python
import jax
import jax.numpy as jnp
from jax import lax
from jax.sharding import PartitionSpec as P


def normalize_axis(values, axis):
    mean = jnp.mean(values, axis=axis, keepdims=True)
    centered = values - mean
    variance = jnp.mean(centered * centered, axis=axis, keepdims=True)
    return centered / jnp.sqrt(variance + 1e-05)


def project(field, w_inputs, w_gate):
    width = w_inputs.shape[1] // 4
    normed = normalize_axis(field, 2).astype(jnp.bfloat16)
    proj = jnp.einsum("rjd,dh->hrj", normed, w_inputs, preferred_element_type=jnp.float32)
    left = (jax.nn.sigmoid(proj[width : 2 * width]) * proj[:width]).astype(jnp.bfloat16)
    right = (jax.nn.sigmoid(proj[3 * width :]) * proj[2 * width : 3 * width]).astype(jnp.bfloat16)
    gating = jax.nn.sigmoid(
        jnp.einsum("rjd,de->rje", normed, w_gate, preferred_element_type=jnp.float32)
    )
    return (left, right, gating)


def finish(field, product, gating, w_final):
    regrouped = lax.all_to_all(product, "ch", split_axis=2, concat_axis=0, tiled=True)
    product_normed = normalize_axis(regrouped, 0).astype(jnp.bfloat16)
    update = jnp.einsum("hrj,hd->rjd", product_normed, w_final, preferred_element_type=jnp.float32)
    return field + gating * update


def body(pair, out_inputs, out_gate, out_final, in_inputs, in_gate, in_final):
    left, right, gating = project(pair, out_inputs, out_gate)
    left_spread, right_spread = (
        lax.all_to_all(left, "ch", split_axis=0, concat_axis=2, tiled=True),
        lax.all_to_all(right, "ch", split_axis=0, concat_axis=2, tiled=True),
    )
    product = jnp.einsum(
        "cik,cjk->cij",
        left_spread,
        lax.all_gather(right_spread, "row", axis=1, tiled=True),
        preferred_element_type=jnp.float32,
    )
    middle = finish(pair, product, gating, out_final)
    left, right, gating = project(middle, in_inputs, in_gate)
    left_spread, right_spread = (
        lax.all_to_all(left, "ch", split_axis=0, concat_axis=2, tiled=True),
        lax.all_to_all(right, "ch", split_axis=0, concat_axis=2, tiled=True),
    )
    right_cols = lax.all_to_all(right_spread, "row", split_axis=2, concat_axis=1, tiled=True)
    product_cols = jnp.einsum(
        "cki,ckj->cij",
        lax.all_gather(left_spread, "row", axis=1, tiled=True),
        right_cols,
        preferred_element_type=jnp.float32,
    )
    product = lax.all_to_all(
        product_cols.astype(jnp.bfloat16), "row", split_axis=1, concat_axis=2, tiled=True
    ).astype(product_cols.dtype)
    return finish(middle, product, gating, in_final)


def solution(mesh):
    placed = (P("row", "ch", None), P(), P(), P(), P(), P(), P())
    return jax.shard_map(
        body, mesh=mesh, in_specs=placed, out_specs=P("row", "ch", None), check_vma=False
    )
```

profile of v0, /device:TPU:1, one launch (start us, length us, event | category | flops | bytes accessed | tf_op | source)
XLA Modules:
  0.0 287.3 jit_solution(1271839749052361159)
XLA Ops:
  6.5 1.1 reduce_sum.72
  7.7 1.2 multiply_reduce_fusion.1
  8.9 1.3 convolution_bitcast_fusion.1
  11.3 28.5 %all_to_all.135 = bf16[16,2,2048]{2,1,0:T(2,128)(2,1)S(1)} all-to-all(bf16[16,2,2048]{2,1,0:T(2,128)(2,1)S(1)} %reshape.62), channel_id=1, replica_groups=mesh['row'=32,'ch'=16] {'ch'}, dimensions={0} | all-to-all | bytes 262144 | tf_op jit(solution)/shard_map/all_to_all | solution.py:37
  40.4 1.1 all_to_all.105
  42.5 15.1 %all_to_all.136 = bf16[16,2,2048]{2,1,0:T(2,128)(2,1)S(1)} all-to-all(bf16[16,2,2048]{2,1,0:T(2,128)(2,1)S(1)} %reshape.60), channel_id=1, replica_groups=mesh['row'=32,'ch'=16] {'ch'}, dimensions={0} | all-to-all | bytes 262144 | tf_op jit(solution)/shard_map/all_to_all | solution.py:36
  58.8 44.5 %all-gather.3.cloned.1.call-done = bf16[8,512,512]{2,1,0:T(8,128)(2,1)} async-done(((bf16[8,16,512]{2,1,0:T(8,128)(2,1)}), bf16[8,512,512]{2,1,0:T(8,128)(2,1)}) %all-gather.3.cloned.1.call-update) | async-done | bytes 4194320 | tf_op jit(solution)/shard_map/all_gather | solution.py:42
  103.3 3.4 %fusion.41 = f32[8,16,512]{2,1,0:T(8,128)S(1)} fusion(bf16[8,16,512]{2,1,0:T(8,128)(2,1)S(1)} %all_to_all.101, bf16[8,512,512]{2,1,0:T(8,128)(2,1)} %all-gather.3.cloned.1.call-done), kind=kOutput, calls=%fused_computation.74 | convolution fusion | flops 67108864 | bytes 4587520 | tf_op jit(solution)/shard_map/cik,cjk->cij/dot_general | solution.py:39
  107.4 1.4 reshape.64
  108.9 10.4 %all-to-all-start.2 = ((f32[16,1,4096]{2,1,0:T(1,128)}), f32[16,1,4096]{2,1,0:T(1,128)S(1)}, u32[]{:S(2)}, u32[]{:S(2)}) async-start(f32[16,1,4096]{2,1,0:T(1,128)} %reshape.64), calls=%async_computation.2 | async-start | bytes 524288 | tf_op jit(solution)/shard_map/all_to_all | solution.py:27
  120.4 14.0 %all-to-all-done.2 = f32[16,1,4096]{2,1,0:T(1,128)S(1)} async-done(((f32[16,1,4096]{2,1,0:T(1,128)}), f32[16,1,4096]{2,1,0:T(1,128)S(1)}, u32[]{:S(2)}, u32[]{:S(2)}) %all-to-all-start.2) | async-done | bytes 262176 | tf_op jit(solution)/shard_map/all_to_all | solution.py:27
  134.9 1.2 reduce.4
  137.9 1.4 fusion.40
  141.1 16.5 %all_to_all.137 = bf16[16,2,2048]{2,1,0:T(2,128)(2,1)S(1)} all-to-all(bf16[16,2,2048]{2,1,0:T(2,128)(2,1)S(1)} %reshape.70), channel_id=1, replica_groups=mesh['row'=32,'ch'=16] {'ch'}, dimensions={0} | all-to-all | bytes 262144 | tf_op jit(solution)/shard_map/all_to_all | solution.py:48
  158.2 1.1 all_to_all.113
  160.3 15.1 %all_to_all.138 = bf16[16,2,2048]{2,1,0:T(2,128)(2,1)S(1)} all-to-all(bf16[16,2,2048]{2,1,0:T(2,128)(2,1)S(1)} %reshape.66), channel_id=1, replica_groups=mesh['row'=32,'ch'=16] {'ch'}, dimensions={0} | all-to-all | bytes 262144 | tf_op jit(solution)/shard_map/all_to_all | solution.py:49
  176.3 1.1 reshape.68
  177.4 18.4 %all_to_all.139 = bf16[32,2,1024]{2,1,0:T(2,128)(2,1)S(1)} all-to-all(bf16[32,2,1024]{2,1,0:T(2,128)(2,1)S(1)} %reshape.68), channel_id=1, replica_groups=mesh['row'=32,'ch'=16] {'row'}, dimensions={0} | all-to-all | bytes 262144 | tf_op jit(solution)/shard_map/all_to_all | solution.py:51
  197.2 1.8 all_to_all.121
  199.0 22.1 %all-gather.5.cloned.1.call-done = bf16[8,512,512]{2,1,0:T(8,128)(2,1)} async-done(((bf16[8,16,512]{2,1,0:T(8,128)(2,1)}), bf16[8,512,512]{2,1,0:T(8,128)(2,1)}) %all-gather.5.cloned.1.call-update) | async-done | bytes 4194320 | tf_op jit(solution)/shard_map/all_gather | solution.py:54
  221.1 2.8 convolution_convert_fusion
  224.7 1.1 reshape.72
  225.8 13.8 %all_to_all.140 = bf16[32,2,1024]{2,1,0:T(2,128)(2,1)S(1)} all-to-all(bf16[32,2,1024]{2,1,0:T(2,128)(2,1)S(1)} %reshape.72), channel_id=1, replica_groups=mesh['row'=32,'ch'=16] {'row'}, dimensions={0} | all-to-all | bytes 262144 | tf_op jit(solution)/shard_map/all_to_all | solution.py:58
  241.8 2.6 copy.71
  244.4 3.0 %reshape.74 = f32[16,1,4096]{2,1,0:T(1,128)} reshape(f32[512,8,16]{2,1,0:T(8,128)} %bitcast.103) | data formatting | bytes 524288
  247.4 10.1 %all-to-all-start.7 = ((f32[16,1,4096]{2,1,0:T(1,128)}), f32[16,1,4096]{2,1,0:T(1,128)S(1)}, u32[]{:S(2)}, u32[]{:S(2)}) async-start(f32[16,1,4096]{2,1,0:T(1,128)} %reshape.74), calls=%async_computation.7 | async-start | bytes 524288 | tf_op jit(solution)/shard_map/all_to_all | solution.py:27
  257.6 1.1 fusion.4
  258.6 13.8 %all-to-all-done.7 = f32[16,1,4096]{2,1,0:T(1,128)S(1)} async-done(((f32[16,1,4096]{2,1,0:T(1,128)}), f32[16,1,4096]{2,1,0:T(1,128)S(1)}, u32[]{:S(2)}, u32[]{:S(2)}) %all-to-all-start.7) | async-done | bytes 262176 | tf_op jit(solution)/shard_map/all_to_all | solution.py:27
  272.4 1.2 reduce.5
  274.4 1.6 copy.66
  277.1 1.4 fusion.11
  278.5 2.0 fusion
  (65 shorter events, 18.2 us)
Async XLA Ops:
  6.5 2.4 copy-start
  6.5 96.7 %all-gather.3.cloned.1.call-start = ((), (), s32[]{:S(2)}) async-start(), calls=%async_computation.8 | async-start | bytes 4325376 | tf_op jit(solution)/shard_map/all_gather | solution.py:42
  58.7 60.6 %copy-start.1 = (f32[16,32,128]{2,1,0:T(8,128)S(1)}, f32[16,32,128]{2,1,0:T(8,128)}, u32[]{:S(2)}) copy-start(f32[16,32,128]{2,1,0:T(8,128)} %param.7) | copy-start | bytes 786436
  58.7 60.6 %copy-start.5 = (bf16[128,128]{1,0:T(8,128)(2,1)S(1)}, bf16[128,128]{1,0:T(8,128)(2,1)}, u32[]{:S(2)}) copy-start(bf16[128,128]{1,0:T(8,128)(2,1)} %param.9) | copy-start | bytes 98308
  108.9 25.5 %all-to-all-start.2 = ((f32[16,1,4096]{2,1,0:T(1,128)}), f32[16,1,4096]{2,1,0:T(1,128)S(1)}, u32[]{:S(2)}, u32[]{:S(2)}) async-start(f32[16,1,4096]{2,1,0:T(1,128)} %reshape.64), calls=%async_computation.2 | async-start | bytes 524288 | tf_op jit(solution)/shard_map/all_to_all | solution.py:27
  119.3 101.8 %all-gather.5.cloned.1.call-start = ((), (), s32[]{:S(2)}) async-start(), calls=%async_computation.9 | async-start | bytes 4325376 | tf_op jit(solution)/shard_map/all_gather | solution.py:54
  137.4 2.2 copy-start.4
  139.3 118.2 %copy-start.2 = (f32[16,32,128]{2,1,0:T(8,128)}, f32[16,32,128]{2,1,0:T(8,128)S(1)}, u32[]{:S(2)}) copy-start(f32[16,32,128]{2,1,0:T(8,128)S(1)} %get-tuple-element.10) | copy-start | bytes 786436
  241.1 16.4 %copy-start.6 = (bf16[128,128]{1,0:T(8,128)(2,1)S(1)}, bf16[128,128]{1,0:T(8,128)(2,1)}, u32[]{:S(2)}) copy-start(bf16[128,128]{1,0:T(8,128)(2,1)} %param.12) | copy-start | bytes 98308
  247.4 25.0 %all-to-all-start.7 = ((f32[16,1,4096]{2,1,0:T(1,128)}), f32[16,1,4096]{2,1,0:T(1,128)S(1)}, u32[]{:S(2)}, u32[]{:S(2)}) async-start(f32[16,1,4096]{2,1,0:T(1,128)} %reshape.74), calls=%async_computation.7 | async-start | bytes 524288 | tf_op jit(solution)/shard_map/all_to_all | solution.py:27
  276.0 2.5 copy-start.3
Sparse Core Ops, SparseCore 0:
  41.7 61.5 all-gather.2
  159.4 61.6 all-gather.4
where the time goes:
time: 288 us; the launch traced here: 287 us
  blocking collectives  107 us (37%)
  waiting for transfers between devices  94.4 us (33%)
  local copies, waits for them, and re-layouts  30.3 us (11%)
  starting transfers between devices  20.6 us (7%)
  between operations  13.9 us (5%)
  matrix products  13.3 us (5%)
  other arithmetic  7.44 us (3%)
    all_gather x1, waiting for transfers between devices, body(): lax.all_gather(right_spread, 'row', axis=1, tiled=True)  44.5 us
    all_to_all x2, blocking collectives, body(): lax.all_to_all(right, 'ch', split_axis=0, concat_axis=2, tiled=True)  43.6 us
    all_to_all x2, blocking collectives, body(): lax.all_to_all(left, 'ch', split_axis=0, concat_axis=2, tiled=True)  31.6 us
    all_to_all x2, waiting for transfers between devices, finish(): lax.all_to_all(product, 'ch', split_axis=2, concat_axis=0, tiled=True)  27.7 us
    all_gather x1, waiting for transfers between devices, body(): lax.all_gather(left_spread, 'row', axis=1, tiled=True)  22.1 us
    all_to_all x2, starting transfers between devices, finish(): lax.all_to_all(product, 'ch', split_axis=2, concat_axis=0, tiled=True)  20.5 us
    all_to_all x1, blocking collectives, body(): lax.all_to_all(right_spread, 'row', split_axis=2, concat_axis=1, tiled=True)  18.4 us
    all_to_all x1, blocking collectives, body(): lax.all_to_all(product_cols.astype(jnp.bfloat16), 'row', split_axis=1, co...  13.8 us
  transfers between devices with their start and end apart: 4, of which 4 were waited for; matrix products, arithmetic and copies ran while one was open for 3% of the time, Pallas kernels for 0%

commit v1 on v0

v1 whole, which is shorter than its diff:
```python
import jax
import jax.numpy as jnp
from jax import lax
from jax.experimental import pallas as pl
from jax.experimental.pallas import tpu as pltpu
from jax.sharding import PartitionSpec as P

MESH = pl.DeviceIdType.MESH
BF16 = jnp.bfloat16
F32 = jnp.float32
Y = 8
ROWS = 32
OWNERS = 16
PHASES = 10


def norm0(values):
    mean = jnp.mean(values, axis=0, keepdims=True)
    centered = values - mean
    variance = jnp.mean(centered * centered, axis=0, keepdims=True)
    return centered * lax.rsqrt(variance + 1e-05)


def flip(w):
    return w.astype(F32).T.astype(BF16)


def place(row):
    return pl.multiple_of((row // 2 % 2) * 256 + (row // 4) * 32 + (row % 2) * 16, 16)


def owner_row(m):
    x = m // 4
    return x * 8 + (2 * (m % 2) + x % 2) * 2


def owner_half(m):
    return m % 4 // 2


def kernel(
    z_ref, wi0, wg0, wf0, wi1, wg1, wf1, u_ref,
    z_send, z_got, wi_t, wg_t, wf_t, zt, acc, gate,
    b1_send, b1_got, turn, b2_send, operands, x_send, c1_got, c2_send, c2_got,
    u_send, u_got, size63, send_sem, recv_sem,
):
    row = lax.axis_index("row")
    ch = lax.axis_index("ch")
    y = ch // 2
    half = ch % 2
    x_pos, zlo = row // 8, row % 8 // 2
    mine = x_pos * 4 + half * 2 + zlo // 2
    is_owner = jnp.logical_and(row % 2 == 0, zlo % 2 == x_pos % 2)
    slot = row * 2 + half

    def send(phase, src, dst, to_row, to_ch):
        pltpu.make_async_remote_copy(
            src_ref=src, dst_ref=dst, send_sem=send_sem.at[phase], recv_sem=recv_sem.at[phase],
            device_id=(to_row, to_ch), device_id_type=MESH,
        ).start()

    def keep(phase, src, dst):
        pltpu.make_async_copy(src, dst, recv_sem.at[phase]).start()

    def arrive(phase, ref):
        pltpu.make_async_copy(ref, ref, recv_sem.at[phase]).wait()

    def leave(phase, ref):
        pltpu.make_async_copy(ref, ref, send_sem.at[phase]).wait()

    def over_y(phase, src_of, dst):
        for step in range(1, Y):
            peer = (y + step) % Y
            send(phase, src_of(peer), dst, row, peer * 2 + half)
        keep(phase, src_of(y), dst)

    def swap(src, dst_of):
        for part in range(2):
            lanes = slice(part * 128, part * 128 + 128)
            turn[part] = src[:, :, lanes].astype(F32).reshape(256, 128)
            for b in range(16):
                dst_of(b)[:, lanes] = turn.at[part][pl.ds(b, 16, stride=16), :].astype(BF16)

    barrier = pltpu.get_barrier_semaphore()

    def greet(to_row, to_ch):
        pl.semaphore_signal(barrier, inc=1, device_id=(to_row, to_ch), device_id_type=MESH)

    for step in range(1, Y):
        greet(row, (y + step) % Y * 2 + half)

    @pl.when(is_owner)
    def _():
        def one(step, carry):
            peer = (slot + step) % 64
            greet(peer // 2, y * 2 + peer % 2)
            return carry

        lax.fori_loop(1, 64, one, 0)

    @pl.when(jnp.logical_not(is_owner))
    def _():
        for m in range(OWNERS):
            greet(owner_row(m), y * 2 + owner_half(m))

    z_send[...] = z_ref[...].astype(BF16)

    @pl.when(is_owner)
    def _():
        pl.semaphore_wait(barrier, Y - 1 + 63)

    @pl.when(jnp.logical_not(is_owner))
    def _():
        pl.semaphore_wait(barrier, Y - 1 + OWNERS)

    over_y(
        0,
        lambda peer: z_send.at[pl.ds(peer * 2, 2)],
        z_got.at[:, pl.ds(pl.multiple_of(y * 32, 32), 32), :],
    )
    for u, (wi, wg, wf) in enumerate(((wi0, wg0, wf0), (wi1, wg1, wf1))):
        wi_t[u] = flip(wi[...])
        wg_t[u] = flip(wg[...])
        wf_t[u] = flip(wf[...])
    arrive(0, z_got)
    for i in range(2):
        zt[i] = z_got[i].astype(F32).T

    for u in range(2):
        b1, b2, c1, c2 = (1 + 4 * u + n for n in range(4))
        for i in range(2):
            zn = norm0(zt[i]).astype(BF16)
            proj = jnp.dot(wi_t[u], zn, preferred_element_type=F32)
            b1_send[u, 0, i] = (jax.nn.sigmoid(proj[128:256]) * proj[:128]).astype(BF16)
            b1_send[u, 1, i] = (jax.nn.sigmoid(proj[384:]) * proj[256:384]).astype(BF16)
            gate[i] = jax.nn.sigmoid(jnp.dot(wg_t[u], zn, preferred_element_type=F32))
        over_y(
            b1,
            lambda peer: b1_send.at[u, :, :, pl.ds(pl.multiple_of(peer * 16, 16), 16), :],
            b1_got.at[u, :, pl.ds(y * 2, 2)],
        )
        arrive(b1, b1_got.at[u])
        for side in range(2):
            swap(b1_got.at[u, side], lambda c: b2_send.at[u, c, side])

        here = operands.at[
            u, :, pl.ds(place(row), 16), pl.ds(pl.multiple_of(half * 256, 256), 256)
        ]

        def to_owner(step, carry):
            m = (slot + step) % OWNERS
            own = jnp.logical_and(is_owner, m == mine)

            @pl.when(own)
            def _():
                keep(b2, b2_send.at[u, m], here)

            @pl.when(jnp.logical_not(own))
            def _():
                send(b2, b2_send.at[u, m], here, owner_row(m), y * 2 + owner_half(m))

            return carry

        lax.fori_loop(0, OWNERS, to_owner, 0)

        @pl.when(is_owner)
        def _():
            arrive(b2, operands.at[u])

            def part(q, carry):
                rows = pl.ds(pl.multiple_of(q * 128, 128), 128)
                if u == 0:
                    product = lax.dot_general(
                        operands[u, 0, rows, :], operands[u, 1],
                        (((1,), (1,)), ((), ())), preferred_element_type=F32,
                    )
                else:
                    product = lax.dot_general(
                        operands[u, 0, :, rows], operands[u, 1],
                        (((0,), (0,)), ((), ())), preferred_element_type=F32,
                    )
                x_send[u, rows, :] = product.astype(BF16)
                return carry

            lax.fori_loop(0, 4, part, 0)

            def block(peer):
                return x_send.at[
                    u, pl.ds(place(peer // 2), 16),
                    pl.ds(pl.multiple_of(peer % 2 * 256, 256), 256),
                ]

            def back(step, carry):
                peer = (slot + step) % 64
                send(c1, block(peer), c1_got.at[u, mine], peer // 2, y * 2 + peer % 2)
                return carry

            keep(c1, block(slot), c1_got.at[u, mine])
            lax.fori_loop(1, 64, back, 0)

        arrive(c1, c1_got.at[u])
        swap(c1_got.at[u], lambda i: c2_send.at[u, i])
        over_y(
            c2,
            lambda peer: c2_send.at[u, pl.ds(peer * 2, 2)],
            c2_got.at[u, :, pl.ds(pl.multiple_of(y * 16, 16), 16), :],
        )
        arrive(c2, c2_got.at[u])
        for i in range(2):
            xn = norm0(c2_got[u, i].astype(F32)).astype(BF16)
            update = gate[i] * jnp.dot(wf_t[u], xn, preferred_element_type=F32)
            if u == 0:
                acc[i] = update
                zt[i] += update
            else:
                u_send[i] = (acc[i] + update).T.astype(BF16)

    over_y(
        9,
        lambda peer: u_send.at[:, pl.ds(pl.multiple_of(peer * 32, 32), 32), :],
        u_got.at[pl.ds(y * 2, 2)],
    )
    leave(0, z_send.at[pl.ds(0, 14)])
    for u in range(2):
        b1, b2, c1, c2 = (1 + 4 * u + n for n in range(4))
        leave(b1, b1_send.at[u, :, :, pl.ds(0, 112), :])

        @pl.when(is_owner)
        def _():
            leave(b2, b2_send.at[u, pl.ds(0, 15)])
            leave(c1, size63)

        @pl.when(jnp.logical_not(is_owner))
        def _():
            leave(b2, b2_send.at[u])

        leave(c2, c2_send.at[u, pl.ds(0, 14)])
    leave(9, u_send.at[:, pl.ds(0, 224), :])
    arrive(9, u_got)
    u_ref[...] = u_got[...]


def body(pair, out_inputs, out_gate, out_final, in_inputs, in_gate, in_final):
    vmem = pl.BlockSpec(memory_space=pltpu.VMEM)
    total = pl.pallas_call(
        kernel,
        out_shape=jax.ShapeDtypeStruct((16, 32, 128), BF16),
        in_specs=[vmem] * 7,
        out_specs=vmem,
        scratch_shapes=[
            pltpu.VMEM((16, 32, 128), BF16),
            pltpu.VMEM((2, 256, 128), BF16),
            pltpu.VMEM((2, 512, 128), BF16),
            pltpu.VMEM((2, 128, 128), BF16),
            pltpu.VMEM((2, 128, 128), BF16),
            pltpu.VMEM((2, 128, 256), F32),
            pltpu.VMEM((2, 128, 256), F32),
            pltpu.VMEM((2, 128, 256), F32),
            pltpu.VMEM((2, 2, 2, 128, 256), BF16),
            pltpu.VMEM((2, 2, 16, 16, 256), BF16),
            pltpu.VMEM((2, 256, 128), F32),
            pltpu.VMEM((2, 16, 2, 16, 256), BF16),
            pltpu.VMEM((2, 2, 512, 512), BF16),
            pltpu.VMEM((2, 512, 512), BF16),
            pltpu.VMEM((2, 16, 16, 256), BF16),
            pltpu.VMEM((2, 16, 16, 256), BF16),
            pltpu.VMEM((2, 2, 128, 256), BF16),
            pltpu.VMEM((2, 256, 128), BF16),
            pltpu.VMEM((16, 32, 128), BF16),
            pltpu.VMEM((1008, 256), BF16),
            pltpu.SemaphoreType.DMA((PHASES,)),
            pltpu.SemaphoreType.DMA((PHASES,)),
        ],
        compiler_params=pltpu.CompilerParams(
            collective_id=0, has_side_effects=True, vmem_limit_bytes=40 * 1024 * 1024
        ),
        name="triangles",
    )(pair, out_inputs, out_gate, out_final, in_inputs, in_gate, in_final)
    return pair + total.astype(F32)


def solution(mesh):
    placed = (P("row", "ch", None), P(), P(), P(), P(), P(), P())
    return jax.shard_map(
        body, mesh=mesh, in_specs=placed, out_specs=P("row", "ch", None), check_vma=False
    )
```

time: 288 us -> 103 us (0.36)
  blocking collectives: 107 us -> 0 us
  Pallas kernels: 0 us -> 95.3 us
  waiting for transfers between devices: 94.4 us -> 0 us
  local copies, waits for them, and re-layouts: 30.3 us -> 5.79 us
  starting transfers between devices: 20.6 us -> 0 us
  between operations: 13.9 us -> 0.02 us
  matrix products: 13.3 us -> 0 us
  other arithmetic: 7.44 us -> 0.73 us
    all_to_all x6 -> x0, blocking collectives: 107 us -> none  [the longest x2 43.6 us: body(): lax.all_to_all(right, 'ch', split_axis=0, concat_axis=2, tiled=True)]
    pallas_call x0 -> x1, Pallas kernels: none -> 95.3 us  [body(): pl.pallas_call(kernel, out_shape=jax.ShapeDtypeStruct((16, 32, 128), BF16...]
    all_gather x2 -> x0, waiting for transfers between devices: 66.6 us -> none  [the longest x1 44.5 us: body(): lax.all_gather(right_spread, 'row', axis=1, tiled=True)]
    all_to_all x2 -> x0, waiting for transfers between devices: 27.7 us -> none  [finish(): lax.all_to_all(product, 'ch', split_axis=2, concat_axis=0, tiled=True)]
    all_to_all x2 -> x0, starting transfers between devices: 20.5 us -> none  [finish(): lax.all_to_all(product, 'ch', split_axis=2, concat_axis=0, tiled=True)]
    dot_general x8 -> x0, matrix products: 13.3 us -> none  [the longest x1 3.37 us: body(): jnp.einsum('cik,cjk->cij', left_spread, lax.all_gather(right_spread, 'row...]
    all_to_all x14 -> x0, local copies, waits for them, and re-layouts: 11.1 us -> none  [the longest x4 3.61 us: finish(): lax.all_to_all(product, 'ch', split_axis=2, concat_axis=0, tiled=True)]
    unnamed x30 -> x14, local copies, waits for them, and re-layouts: 12.6 us -> 5.79 us
  transfers between devices with their start and end apart: 4 -> 0, of which waited for: 4 -> 0; matrix products, arithmetic and copies ran while one was open for 3% -> 0% of each run, Pallas kernels for 0% -> 0%
where the time goes in v1:
time: 103 us; the launch traced here: 102 us
  Pallas kernels  95.3 us (93%)
  local copies, waits for them, and re-layouts  5.79 us (6%)
    pallas_call x1, Pallas kernels, body(): pl.pallas_call(kernel, out_shape=jax.ShapeDtypeStruct((16, 32, 128), BF16...  95.3 us
    unnamed x14, local copies, waits for them, and re-layouts  5.79 us

profile of v1, /device:TPU:1, one launch (start us, length us, event | category | flops | bytes accessed | tf_op | source)
XLA Modules:
  0.0 101.8 jit_solution(4861224186758159699)
XLA Ops:
  0.0 0.0 copy-start
  0.0 0.9 copy-done
  1.0 0.0 copy-start.1
  1.0 0.9 copy-done.1
  1.9 0.0 copy-start.2
  1.9 0.9 copy-done.2
  2.8 0.0 copy-start.3
  2.8 0.8 copy-done.3
  3.5 0.0 copy-start.4
  3.5 0.8 copy-done.4
  4.3 0.0 copy-start.5
  4.3 0.8 copy-done.5
  5.0 0.0 copy-start.6
  5.0 0.8 copy-done.6
  5.8 95.3 %triangles.1 = bf16[16,32,128]{2,1,0:T(8,128)(2,1)S(1)} custom-call(f32[16,32,128]{2,1,0:T(8,128)S(1)} %copy-done, bf16[128,512]{1,0:T(8,128)(2,1)S(1)} %copy-done.1, bf16[128,128]{1,0:T(8,128)(2,1)S(1)} %copy-done.3, bf16[128,128]{1,0:T(8,128)(2,1)S(1)} %copy-done.4, bf16[128,512]{1,0:T(8,128)(2,1)S(1)} %copy-done.2, bf16[128,128]{1,0:T(8,128)(2,1)S(1)} %copy-done.5, ...), custom_call_target="tpu_custom_call" | custom-call | tf_op jit(solution)/shard_map/triangles/pallas_call | solution.py:245
  101.1 0.7 convert_add_fusion
Async XLA Ops:
  0.0 0.9 copy-start
  1.0 0.9 copy-start.1
  1.9 0.9 copy-start.2
  2.8 0.8 copy-start.3
  3.5 0.8 copy-start.4
  4.3 0.8 copy-start.5
  5.0 0.8 copy-start.6

commit v2 on v0

v2 whole, which is shorter than its diff:
```python
import jax
import jax.numpy as jnp
from jax import lax
from jax.experimental import pallas as pl
from jax.experimental.pallas import tpu as pltpu
from jax.sharding import PartitionSpec as P

MESH = pl.DeviceIdType.MESH
BF16 = jnp.bfloat16
F32 = jnp.float32
GROUP = 8
OWNERS = 16
PHASES = 10


def norm0(values):
    mean = jnp.mean(values, axis=0, keepdims=True)
    centered = values - mean
    variance = jnp.mean(centered * centered, axis=0, keepdims=True)
    return centered * lax.rsqrt(variance + 1e-05)


def flip(w):
    return w.astype(F32).T.astype(BF16)


def place(zlo, y):
    return pl.multiple_of(zlo * 128 + y * 16, 16)


def runs(chunk):
    for y in range(chunk, 8, 2):
        for high in range(2):
            for low in range(2):
                yield y * 32 + high * 16 + low, y // 2 * 4 + high * 2 + low


def kernel(
    z_hbm, wi0, wg0, wf0, wi1, wg1, wf1, u_ref,
    z_in, wi_in, wg_in, wf_in, z_send, z_got, wi_t, wg_t, wf_t, zt, acc, gate,
    b1_send, b1_got, natural_rows, ordered_rows, turn, b2_send, operands, x_send,
    c1_got, c2_send, c2_got, u_send, u_got, size63, send_sem, recv_sem, in_sem,
):
    row = lax.axis_index("row")
    ch = lax.axis_index("ch")
    y, zhi = ch // 2, ch % 2
    x, zlo, core = row // 8, row % 8 // 2, row % 2
    g = x * 2 + core

    def owner_zlo(m):
        return m // 2 % 2 + 2 * ((m // 4 + core) % 2)

    def plane(peer_zlo):
        return x * 8 + peer_zlo * 2 + core

    is_owner = zlo == owner_zlo(ch)

    def send(phase, chunk, src, dst, to_row, to_ch):
        pltpu.make_async_remote_copy(
            src_ref=src, dst_ref=dst,
            send_sem=send_sem.at[phase], recv_sem=recv_sem.at[phase, chunk],
            device_id=(to_row, to_ch), device_id_type=MESH,
        ).start()

    def keep(phase, chunk, src, dst):
        pltpu.make_async_copy(src, dst, recv_sem.at[phase, chunk]).start()

    def arrive(phase, chunk, ref):
        pltpu.make_async_copy(ref, ref, recv_sem.at[phase, chunk]).wait()

    def leave(phase, ref):
        pltpu.make_async_copy(ref, ref, send_sem.at[phase]).wait()

    def y_peer(step):
        peer = (y + step) % GROUP
        return peer, row, peer * 2 + zhi

    def g_peer(step):
        peer = (g + step) % GROUP
        return peer, peer // 2 * 8 + zlo * 2 + peer % 2, ch

    def z_peer(step):
        peer = (zhi * 4 + zlo + step) % GROUP
        return peer, plane(peer % 4), y * 2 + peer // 4

    def spread(phase, chunk, peer_of, src_of, dst):
        for step in range(1, GROUP):
            peer, to_row, to_ch = peer_of(step)
            send(phase, chunk, src_of(peer), dst, to_row, to_ch)
        keep(phase, chunk, src_of(peer_of(0)[0]), dst)

    def swap(src, dst_of):
        turn[...] = src[...].astype(F32).reshape(256, 128)
        for b in range(16):
            dst_of(b)[...] = turn[pl.ds(b, 16, stride=16), :].astype(BF16)

    weights = ((wi0, wi_in.at[0]), (wg0, wg_in.at[0]), (wf0, wf_in.at[0]),
               (wi1, wi_in.at[1]), (wg1, wg_in.at[1]), (wf1, wf_in.at[1]))
    loads = [
        pltpu.make_async_copy(src, dst, in_sem.at[n])
        for n, (src, dst) in enumerate(((z_hbm, z_in), *weights))
    ]
    for load in loads:
        load.start()

    barrier = pltpu.get_barrier_semaphore()
    for line in (y_peer, g_peer, z_peer):
        for step in range(1, GROUP):
            _, to_row, to_ch = line(step)
            pl.semaphore_signal(
                barrier, inc=1, device_id=(to_row, to_ch), device_id_type=MESH
            )
    loads[0].wait()
    z_send[...] = z_in[...].astype(BF16)
    pl.semaphore_wait(barrier, 3 * (GROUP - 1))

    spread(
        0, 0, y_peer,
        lambda peer: z_send.at[pl.ds(peer * 2, 2)],
        z_got.at[:, pl.ds(pl.multiple_of(y * 32, 32), 32), :],
    )
    for load in loads[1:]:
        load.wait()
    for u in range(2):
        wi_t[u] = flip(wi_in[u])
        wg_t[u] = flip(wg_in[u])
        wf_t[u] = flip(wf_in[u])
    arrive(0, 0, z_got)

    def project(u, chunk, field):
        zn = norm0(field).astype(BF16)
        proj = jnp.dot(wi_t[u], zn, preferred_element_type=F32)
        left = (jax.nn.sigmoid(proj[128:256]) * proj[:128]).astype(BF16)
        right = (jax.nn.sigmoid(proj[384:]) * proj[256:384]).astype(BF16)
        for i in range(2):
            b1_send[u, chunk, 0, i] = left[:, i * 128:i * 128 + 128]
            b1_send[u, chunk, 1, i] = right[:, i * 128:i * 128 + 128]
        spread(
            1 + 4 * u, chunk, g_peer,
            lambda peer: b1_send.at[
                u, chunk, :, :, pl.ds(pl.multiple_of(peer * 16, 16), 16), :
            ],
            b1_got.at[u, chunk, :, pl.ds(g * 2, 2)],
        )
        gate[chunk] = jax.nn.sigmoid(jnp.dot(wg_t[u], zn, preferred_element_type=F32))

    for chunk in range(2):
        for i in range(2):
            natural_rows[...] = z_got[i].astype(F32)
            for natural, ordered in runs(chunk):
                ordered_rows[pl.ds(ordered, 8, stride=16), :] = natural_rows[
                    pl.ds(natural, 8, stride=2), :
                ]
            zt[chunk, :, i * 128:i * 128 + 128] = ordered_rows[...].T
        project(0, chunk, zt[chunk])

    for u in range(2):
        b1, b2, c1, c2 = (1 + 4 * u + n for n in range(4))
        for chunk in range(2):
            arrive(b1, chunk, b1_got.at[u, chunk])
            for side in range(2):
                swap(b1_got.at[u, chunk, side], lambda c: b2_send.at[u, chunk, c, side])
            here = operands.at[
                u, :, pl.ds(place(zlo, y), 16),
                pl.ds(pl.multiple_of(chunk * 256 + zhi * 128, 128), 128),
            ]
            for step in range(1, OWNERS):
                m = (ch + step) % OWNERS
                send(b2, chunk, b2_send.at[u, chunk, m], here, plane(owner_zlo(m)), m)

            @pl.when(is_owner)
            def _():
                keep(b2, chunk, b2_send.at[u, chunk, ch], here)

            @pl.when(jnp.logical_not(is_owner))
            def _():
                send(b2, chunk, b2_send.at[u, chunk, ch], here, plane(owner_zlo(ch)), ch)

        @pl.when(is_owner)
        def _():
            for chunk in range(2):
                arrive(b2, chunk, operands.at[u, :, :, pl.ds(chunk * 256, 256)])
            for chunk in range(2):
                mine = c1_got.at[u, chunk, ch]

                def back(step, carry):
                    peer_zlo = (zlo + step) % 4
                    rows = pl.ds(pl.multiple_of(peer_zlo * 128, 128), 128)
                    columns = pl.ds(chunk * 256, 256)
                    if u == 0:
                        product = lax.dot_general(
                            operands[u, 0, rows, :], operands[u, 1, columns, :],
                            (((1,), (1,)), ((), ())), preferred_element_type=F32,
                        )
                    else:
                        product = lax.dot_general(
                            operands[u, 0, :, rows], operands[u, 1, :, columns],
                            (((0,), (0,)), ((), ())), preferred_element_type=F32,
                        )
                    x_send[u, chunk, rows, :] = product.astype(BF16)

                    def block(peer_ch):
                        return x_send.at[
                            u, chunk, pl.ds(place(peer_zlo, peer_ch // 2), 16),
                            pl.ds(pl.multiple_of(peer_ch % 2 * 128, 128), 128),
                        ]

                    for other in range(1, 16):
                        peer_ch = (ch + other) % 16
                        send(c1, chunk, block(peer_ch), mine, plane(peer_zlo), peer_ch)

                    @pl.when(peer_zlo == zlo)
                    def _():
                        keep(c1, chunk, block(ch), mine)

                    @pl.when(peer_zlo != zlo)
                    def _():
                        send(c1, chunk, block(ch), mine, plane(peer_zlo), ch)

                    return carry

                lax.fori_loop(1, 5, back, 0)

        for chunk in range(2):
            arrive(c1, chunk, c1_got.at[u, chunk])
            swap(c1_got.at[u, chunk], lambda i: c2_send.at[u, chunk, i])
            spread(
                c2, chunk, g_peer,
                lambda peer: c2_send.at[u, chunk, pl.ds(peer * 2, 2)],
                c2_got.at[u, chunk, :, pl.ds(pl.multiple_of(g * 16, 16), 16), :],
            )
        for chunk in range(2):
            arrive(c2, chunk, c2_got.at[u, chunk])
            product = jnp.concatenate(
                [c2_got[u, chunk, i].astype(F32) for i in range(2)], axis=1
            )
            update = gate[chunk] * jnp.dot(
                wf_t[u], norm0(product).astype(BF16), preferred_element_type=F32
            )
            if u == 0:
                acc[chunk] = update
                project(1, chunk, zt[chunk] + update)
                continue
            total = acc[chunk] + update
            for i in range(2):
                ordered_rows[...] = total[:, i * 128:i * 128 + 128].T
                for natural, ordered in runs(chunk):
                    natural_rows[pl.ds(natural, 8, stride=2), :] = ordered_rows[
                        pl.ds(ordered, 8, stride=16), :
                    ]
                for part in range(chunk, 8, 2):
                    there = slice(part * 32, part * 32 + 32)
                    u_send[i, there, :] = natural_rows[there, :].astype(BF16)
            home = u_got.at[pl.ds(y * 2, 2)]

            def columns_of(peer):
                return u_send.at[:, pl.ds(pl.multiple_of(peer * 32, 32), 32), :]

            for step in range(1, 4):
                peer = (y // 2 + step) % 4 * 2 + chunk
                send(9, 0, columns_of(peer), home, row, peer * 2 + zhi)

            @pl.when(y % 2 == chunk)
            def _():
                keep(9, 0, columns_of(y), home)

            @pl.when(y % 2 != chunk)
            def _():
                peer = y // 2 * 2 + chunk
                send(9, 0, columns_of(peer), home, row, peer * 2 + zhi)

    leave(0, z_send.at[pl.ds(0, 14)])
    for u in range(2):
        b1, b2, c1, c2 = (1 + 4 * u + n for n in range(4))
        leave(b1, b1_send.at[u, :, :, :, pl.ds(0, 112), :])

        @pl.when(is_owner)
        def _():
            leave(b2, b2_send.at[u, :, pl.ds(0, 15)])
            leave(c1, size63)

        @pl.when(jnp.logical_not(is_owner))
        def _():
            leave(b2, b2_send.at[u])

        leave(c2, c2_send.at[u, :, pl.ds(0, 14)])
    leave(9, u_send.at[:, pl.ds(0, 224), :])
    arrive(9, 0, u_got)
    u_ref[...] = u_got[...]


def body(pair, out_inputs, out_gate, out_final, in_inputs, in_gate, in_final):
    anywhere = pl.BlockSpec(memory_space=pl.ANY)
    total = pl.pallas_call(
        kernel,
        out_shape=jax.ShapeDtypeStruct((16, 32, 128), BF16),
        in_specs=[anywhere] * 7,
        out_specs=pl.BlockSpec(memory_space=pltpu.VMEM),
        scratch_shapes=[
            pltpu.VMEM((16, 32, 128), F32),
            pltpu.VMEM((2, 128, 512), BF16),
            pltpu.VMEM((2, 128, 128), BF16),
            pltpu.VMEM((2, 128, 128), BF16),
            pltpu.VMEM((16, 32, 128), BF16),
            pltpu.VMEM((2, 256, 128), BF16),
            pltpu.VMEM((2, 512, 128), BF16),
            pltpu.VMEM((2, 128, 128), BF16),
            pltpu.VMEM((2, 128, 128), BF16),
            pltpu.VMEM((2, 128, 256), F32),
            pltpu.VMEM((2, 128, 256), F32),
            pltpu.VMEM((2, 128, 256), F32),
            pltpu.VMEM((2, 2, 2, 2, 128, 128), BF16),
            pltpu.VMEM((2, 2, 2, 16, 16, 128), BF16),
            pltpu.VMEM((256, 128), F32),
            pltpu.VMEM((128, 128), F32),
            pltpu.VMEM((256, 128), F32),
            pltpu.VMEM((2, 2, 16, 2, 16, 128), BF16),
            pltpu.VMEM((2, 2, 512, 512), BF16),
            pltpu.VMEM((2, 2, 512, 256), BF16),
            pltpu.VMEM((2, 2, 16, 16, 128), BF16),
            pltpu.VMEM((2, 2, 16, 16, 128), BF16),
            pltpu.VMEM((2, 2, 2, 128, 128), BF16),
            pltpu.VMEM((2, 256, 128), BF16),
            pltpu.VMEM((16, 32, 128), BF16),
            pltpu.VMEM((1008, 256), BF16),
            pltpu.SemaphoreType.DMA((PHASES,)),
            pltpu.SemaphoreType.DMA((PHASES, 2)),
            pltpu.SemaphoreType.DMA((7,)),
        ],
        compiler_params=pltpu.CompilerParams(
            collective_id=0, has_side_effects=True, vmem_limit_bytes=60 * 1024 * 1024
        ),
        name="triangles",
    )(pair, out_inputs, out_gate, out_final, in_inputs, in_gate, in_final)
    return pair + total.astype(F32)


def solution(mesh):
    placed = (P("row", "ch", None), P(), P(), P(), P(), P(), P())
    return jax.shard_map(
        body, mesh=mesh, in_specs=placed, out_specs=P("row", "ch", None), check_vma=False
    )
```

time: 288 us -> 87.8 us (0.30)
  blocking collectives: 107 us -> 0 us
  waiting for transfers between devices: 94.4 us -> 0 us
  Pallas kernels: 0 us -> 86 us
  local copies, waits for them, and re-layouts: 30.3 us -> 0.01 us
  starting transfers between devices: 20.6 us -> 0 us
  between operations: 13.9 us -> 0.02 us
  matrix products: 13.3 us -> 0 us
  other arithmetic: 7.44 us -> 1.64 us
    all_to_all x6 -> x0, blocking collectives: 107 us -> none  [the longest x2 43.6 us: body(): lax.all_to_all(right, 'ch', split_axis=0, concat_axis=2, tiled=True)]
    pallas_call x0 -> x1, Pallas kernels: none -> 86 us  [body(): pl.pallas_call(kernel, out_shape=jax.ShapeDtypeStruct((16, 32, 128), BF16...]
    all_gather x2 -> x0, waiting for transfers between devices: 66.6 us -> none  [the longest x1 44.5 us: body(): lax.all_gather(right_spread, 'row', axis=1, tiled=True)]
    all_to_all x2 -> x0, waiting for transfers between devices: 27.7 us -> none  [finish(): lax.all_to_all(product, 'ch', split_axis=2, concat_axis=0, tiled=True)]
    all_to_all x2 -> x0, starting transfers between devices: 20.5 us -> none  [finish(): lax.all_to_all(product, 'ch', split_axis=2, concat_axis=0, tiled=True)]
    dot_general x8 -> x0, matrix products: 13.3 us -> none  [the longest x1 3.37 us: body(): jnp.einsum('cik,cjk->cij', left_spread, lax.all_gather(right_spread, 'row...]
    unnamed x30 -> x2, local copies, waits for them, and re-layouts: 12.6 us -> 0.01 us
    all_to_all x14 -> x0, local copies, waits for them, and re-layouts: 11.1 us -> none  [the longest x4 3.61 us: finish(): lax.all_to_all(product, 'ch', split_axis=2, concat_axis=0, tiled=True)]
  transfers between devices with their start and end apart: 4 -> 0, of which waited for: 4 -> 0; matrix products, arithmetic and copies ran while one was open for 3% -> 0% of each run, Pallas kernels for 0% -> 0%
where the time goes in v2:
time: 87.8 us; the launch traced here: 87.7 us
  Pallas kernels  86 us (98%)
  other arithmetic  1.64 us (2%)
    pallas_call x1, Pallas kernels, body(): pl.pallas_call(kernel, out_shape=jax.ShapeDtypeStruct((16, 32, 128), BF16...  86 us

profile of v2, /device:TPU:1, one launch (start us, length us, event | category | flops | bytes accessed | tf_op | source)
XLA Modules:
  0.0 87.7 jit_solution(14453592223524436213)
XLA Ops:
  0.0 0.0 copy-start
  0.0 86.0 %triangles.1 = bf16[16,32,128]{2,1,0:T(8,128)(2,1)} custom-call(f32[16,32,128]{2,1,0:T(8,128)} %z_hbm.1, bf16[128,512]{1,0:T(8,128)(2,1)} %wi0.1, bf16[128,128]{1,0:T(8,128)(2,1)} %wg0.1, bf16[128,128]{1,0:T(8,128)(2,1)} %wf0.1, bf16[128,512]{1,0:T(8,128)(2,1)} %wi1.1, bf16[128,128]{1,0:T(8,128)(2,1)} %wg1.1, bf16[128,128]{1,0:T(8,128)(2,1)} %wf1.1), custom_call_target="tpu_custom_call" | custom-call | tf_op jit(solution)/shard_map/triangles/pallas_call | solution.py:294
  86.0 0.0 copy-done
  86.1 1.6 %convert_add_fusion = f32[16,32,128]{2,1,0:T(8,128)} fusion(f32[16,32,128]{2,1,0:T(8,128)S(1)} %copy-done, bf16[16,32,128]{2,1,0:T(8,128)(2,1)} %triangles.1), kind=kLoop, calls=%fused_computation | loop fusion | flops 131072 | bytes 655360 | tf_op jit(solution)/shard_map/add | solution.py:335
Async XLA Ops:
  0.0 86.0 %copy-start = (f32[16,32,128]{2,1,0:T(8,128)S(1)}, f32[16,32,128]{2,1,0:T(8,128)}, u32[]{:S(2)}) copy-start(f32[16,32,128]{2,1,0:T(8,128)} %z_hbm.1) | copy-start | bytes 786436

commit v3 on v2

v3 whole, which is shorter than its diff:
```python
import jax
import jax.numpy as jnp
from jax import lax
from jax.experimental import pallas as pl
from jax.experimental.pallas import tpu as pltpu
from jax.sharding import PartitionSpec as P

MESH = pl.DeviceIdType.MESH
BF16 = jnp.bfloat16
F32 = jnp.float32
GROUP = 8
OWNERS = 16
FAR_FIRST = (4, 3, 5, 2, 6, 1, 7)
PHASES = 10


def norm0(values):
    mean = jnp.mean(values, axis=0, keepdims=True)
    centered = values - mean
    variance = jnp.mean(centered * centered, axis=0, keepdims=True)
    return centered * lax.rsqrt(variance + 1e-05)


def flip(w):
    return w.astype(F32).T.astype(BF16)


def place(zlo, y):
    return pl.multiple_of(zlo * 128 + y * 16, 16)


def kernel(
    z_hbm, wi0, wg0, wf0, wi1, wg1, wf1, out_ref,
    z_in, wi_in, wg_in, wf_in, z_send, z_got, wi_t, wg_t, wf_t, zt, acc, gate,
    h_send, h_got, fan, square, k_send, b1_send, b1_got, turn, b2_send, operands,
    x1_send, c1_got, c2_send, c2_got, x2_send, t1_got, t2_send, t2_got,
    u_send, u_got, middle_t, home_gate, turned, size63, send_sem, recv_sem, in_sem, ready,
):
    row = lax.axis_index("row")
    ch = lax.axis_index("ch")
    y, zhi = ch // 2, ch % 2
    x, zlo, core = row // 8, row % 8 // 2, row % 2
    g = x * 2 + core

    def owner_zlo(m):
        return m // 2 % 2 + 2 * ((m // 4 + core) % 2)

    def plane(peer_zlo):
        return x * 8 + peer_zlo * 2 + core

    is_owner = zlo == owner_zlo(ch)

    def send(phase, chunk, src, dst, to_row, to_ch):
        pltpu.make_async_remote_copy(
            src_ref=src, dst_ref=dst,
            send_sem=send_sem.at[phase], recv_sem=recv_sem.at[phase, chunk],
            device_id=(to_row, to_ch), device_id_type=MESH,
        ).start()

    def keep(phase, chunk, src, dst):
        pltpu.make_async_copy(src, dst, recv_sem.at[phase, chunk]).start()

    def arrive(phase, chunk, ref):
        pltpu.make_async_copy(ref, ref, recv_sem.at[phase, chunk]).wait()

    def leave(phase, ref):
        pltpu.make_async_copy(ref, ref, send_sem.at[phase]).wait()

    def y_peer(step):
        peer = (y + step) % GROUP
        return peer, row, peer * 2 + zhi

    def g_peer(step):
        peer = (g + step) % GROUP
        return peer, peer // 2 * 8 + zlo * 2 + peer % 2, ch

    def z_peer(step):
        peer = (zhi * 4 + zlo + step) % GROUP
        return peer, plane(peer % 4), y * 2 + peer // 4

    def spread(phase, chunk, peer_of, src_of, dst):
        for step in FAR_FIRST:
            peer, to_row, to_ch = peer_of(step)
            send(phase, chunk, src_of(peer), dst, to_row, to_ch)
        keep(phase, chunk, src_of(peer_of(0)[0]), dst)

    def others():
        for dy in (*FAR_FIRST, 0):
            for dz in (1, 0):
                if dy or dz:
                    yield (y + dy) % 8 * 2 + (zhi + dz) % 2

    def to_owners(phase, chunk, src_of, here):
        for m in others():
            send(phase, chunk, src_of(m), here, plane(owner_zlo(m)), m)

        @pl.when(is_owner)
        def _():
            keep(phase, chunk, src_of(ch), here)

        @pl.when(jnp.logical_not(is_owner))
        def _():
            send(phase, chunk, src_of(ch), here, plane(owner_zlo(ch)), ch)

    def both(stage):
        def one(chunk, carry):
            stage(chunk)
            return carry

        lax.fori_loop(0, 2, one, 0)

    def swap(src, dst_of):
        turn[...] = src[...].astype(F32).reshape(256, 128)
        for b in range(16):
            dst_of(b)[...] = turn[pl.ds(b, 16, stride=16), :].astype(BF16)

    def lanes(n, width=128):
        return slice(n * width, (n + 1) * width)

    def glu(proj):
        return (jax.nn.sigmoid(proj[128:]) * proj[:128]).astype(BF16)

    weights = ((wi0, wi_in.at[0]), (wg0, wg_in.at[0]), (wf0, wf_in.at[0]),
               (wi1, wi_in.at[1]), (wg1, wg_in.at[1]), (wf1, wf_in.at[1]))
    loads = [
        pltpu.make_async_copy(src, dst, in_sem.at[n])
        for n, (src, dst) in enumerate(((z_hbm, z_in), *weights))
    ]
    for load in loads:
        load.start()

    barrier = pltpu.get_barrier_semaphore()
    for line in (y_peer, g_peer, z_peer):
        for step in range(1, GROUP):
            _, to_row, to_ch = line(step)
            pl.semaphore_signal(
                barrier, inc=1, device_id=(to_row, to_ch), device_id_type=MESH
            )
    loads[1].wait()
    wi_t[0] = flip(wi_in[0])
    loads[0].wait()
    zn = jnp.concatenate(
        [norm0(z_in[4 * a:4 * a + 4].reshape(128, 128).T).astype(BF16) for a in range(4)],
        axis=1,
    )
    for side in range(2):
        h_send[side] = glu(
            jnp.dot(wi_t[0, lanes(side, 256)], zn, preferred_element_type=F32)
        )
        if side == 0:
            pl.semaphore_wait(barrier, 3 * (GROUP - 1))
            for step in FAR_FIRST:
                _, to_row, to_ch = y_peer(step)
                pl.semaphore_signal(
                    ready, inc=1, device_id=(to_row, to_ch), device_id_type=MESH
                )
        spread(
            1, side, g_peer,
            lambda peer: h_send.at[side, pl.ds(pl.multiple_of(peer * 16, 16), 16), :],
            h_got.at[side, g],
        )
    pl.semaphore_wait(ready, GROUP - 1)

    for side in range(2):
        arrive(1, side, h_got.at[side])
        for a in range(4):
            for peer in range(GROUP):
                fan.at[a][pl.ds(peer, 16, stride=8), :] = h_got[
                    side, peer, :, lanes(a)
                ].astype(F32)
            rows = fan[a].reshape(4, 4, 8, 128)
            for b in range(4):
                i = 4 * a + b
                start, stride = (i // 2 * 16 + i % 2, 2) if side == 0 else (i, 16)
                mixed = jnp.concatenate(
                    [rows[:, t].reshape(32, 128)[:, lanes(b, 32)] for t in range(4)], axis=1
                )
                for q in range(4):
                    square.at[q][pl.ds(start, 8, stride=stride), :] = mixed[lanes(q, 8)]
        for q in range(4):
            k_send[4 * q:4 * q + 4, side] = square[q].T.reshape(4, 32, 128).astype(BF16)
        to_owners(
            2, side, lambda m: k_send.at[m, side],
            operands.at[
                0, side, pl.ds(pl.multiple_of(ch * 32, 32), 32),
                pl.ds(pl.multiple_of(zlo * 128, 128), 128),
            ],
        )

    z_send[...] = z_in[...].astype(BF16)
    spread(
        0, 0, y_peer,
        lambda peer: z_send.at[pl.ds(peer * 2, 2)],
        z_got.at[:, pl.ds(pl.multiple_of(y * 32, 32), 32), :],
    )
    for load in loads[2:]:
        load.wait()
    wi_t[1] = flip(wi_in[1])
    for u in range(2):
        wg_t[u] = flip(wg_in[u])
        wf_t[u] = flip(wf_in[u])

    @pl.when(is_owner)
    def _():
        arrive(2, 0, operands.at[0, 0])
        for q in range(4):
            turned[lanes(q), :] = operands[0, 0, :, lanes(q)].T
        arrive(2, 1, operands.at[0, 1])

        def back(step, carry):
            chunk = step // 4
            peer_zlo = (zlo + 1 + step) % 4
            rows = pl.ds(pl.multiple_of(peer_zlo * 128, 128), 128)
            columns = pl.ds(pl.multiple_of(chunk * 256, 256), 256)
            x1_send[chunk, rows, :] = jnp.dot(
                turned[rows, :], operands[0, 1, :, columns], preferred_element_type=F32
            ).astype(BF16)
            mine = c1_got.at[chunk, ch]

            def block(peer_ch):
                return x1_send.at[
                    chunk, pl.ds(place(peer_zlo, peer_ch // 2), 16),
                    pl.ds(pl.multiple_of(peer_ch % 2 * 128, 128), 128),
                ]

            for peer_ch in others():
                send(3, chunk, block(peer_ch), mine, plane(peer_zlo), peer_ch)

            @pl.when(peer_zlo == zlo)
            def _():
                keep(3, chunk, block(ch), mine)

            @pl.when(peer_zlo != zlo)
            def _():
                send(3, chunk, block(ch), mine, plane(peer_zlo), ch)

            return carry

        lax.fori_loop(0, 8, back, 0)

    arrive(0, 0, z_got)
    for chunk in range(2):
        for i in range(2):
            zt[chunk, :, lanes(i)] = jnp.concatenate(
                [z_got[i, lanes(part, 32), :].astype(F32) for part in range(chunk, 8, 2)],
                axis=0,
            ).T
        gate[chunk] = jax.nn.sigmoid(
            jnp.dot(wg_t[0], norm0(zt[chunk]).astype(BF16), preferred_element_type=F32)
        )

    def regroup(chunk):
        arrive(3, chunk, c1_got.at[chunk])
        swap(c1_got.at[chunk], lambda i: c2_send.at[chunk, i])
        spread(
            4, chunk, g_peer,
            lambda peer: c2_send.at[chunk, pl.ds(peer * 2, 2)],
            c2_got.at[chunk, :, pl.ds(pl.multiple_of(g * 16, 16), 16), :],
        )

    both(regroup)

    def middle(chunk):
        arrive(4, chunk, c2_got.at[chunk])
        product = jnp.concatenate(
            [c2_got[chunk, i].astype(F32) for i in range(2)], axis=1
        )
        acc[chunk] = gate[chunk] * jnp.dot(
            wf_t[0], norm0(product).astype(BF16), preferred_element_type=F32
        )
        normed = norm0(zt[chunk] + acc[chunk]).astype(BF16)
        for side in range(2):
            value = glu(
                jnp.dot(wi_t[1, lanes(side, 256)], normed, preferred_element_type=F32)
            )
            for i in range(2):
                b1_send[chunk, side, i] = value[:, lanes(i)]
        spread(
            5, chunk, g_peer,
            lambda peer: b1_send.at[
                chunk, :, :, pl.ds(pl.multiple_of(peer * 16, 16), 16), :
            ],
            b1_got.at[chunk, :, pl.ds(g * 2, 2)],
        )

    both(middle)

    def second_to_owners(chunk):
        arrive(5, chunk, b1_got.at[chunk])
        for side in range(2):
            swap(b1_got.at[chunk, side], lambda c: b2_send.at[chunk, c, side])
        to_owners(
            6, chunk, lambda m: b2_send.at[chunk, m],
            operands.at[
                1, :, pl.ds(place(zlo, y), 16),
                pl.ds(pl.multiple_of(chunk * 256 + zhi * 128, 128), 128),
            ],
        )

    both(second_to_owners)

    for chunk in range(2):
        for i in range(2):
            total = acc[chunk, :, lanes(i)].T.astype(BF16)
            for k in range(4):
                u_send[i, lanes(2 * k + chunk, 32), :] = total[lanes(k, 32)]
    spread(
        9, 0, y_peer,
        lambda peer: u_send.at[:, pl.ds(pl.multiple_of(peer * 32, 32), 32), :],
        u_got.at[pl.ds(y * 2, 2)],
    )

    @pl.when(is_owner)
    def _():
        for chunk in range(2):
            arrive(6, chunk, operands.at[1, :, :, pl.ds(chunk * 256, 256)])
            for q in (2 * chunk, 2 * chunk + 1):
                turned[lanes(q), :] = operands[1, 1, :, lanes(q)].T
        mine = t1_got.at[ch]
        own = y % 2 * 2 + zhi

        def back(step, carry):
            part = (own + 1 + step) % 4
            rows = pl.ds(pl.multiple_of(part * 128, 128), 128)
            x2_send[rows, :] = jnp.dot(
                turned[rows, :], operands[1, 0], preferred_element_type=F32
            ).astype(BF16)

            def go(peer_zlo, k, is_self=False):
                src = x2_send.at[
                    pl.ds(pl.multiple_of(part * 128 + k * 32, 32), 32),
                    pl.ds(pl.multiple_of(peer_zlo * 128, 128), 128),
                ]
                if is_self:
                    keep(7, 0, src, mine)
                else:
                    send(7, 0, src, mine, plane(peer_zlo),
                         (2 * k + part // 2) * 2 + part % 2)

            for dk in (2, 1, 3, 0):
                for dz in (2, 1, 3, 0):
                    if dk or dz:
                        go((zlo + dz) % 4, (y // 2 + dk) % 4)

            @pl.when(part == own)
            def _():
                go(zlo, y // 2, True)

            @pl.when(part != own)
            def _():
                go(zlo, y // 2)

            return carry

        lax.fori_loop(0, 4, back, 0)

    arrive(9, 0, u_got)
    for a in range(4):
        block = z_in[lanes(a, 4)] + u_got[lanes(a, 4)].astype(F32)
        middle_t[:, lanes(a)] = block.reshape(128, 128).T
    for half in range(2):
        normed = norm0(middle_t[:, lanes(half, 256)]).astype(BF16)
        home_gate[:, lanes(half, 256)] = jax.nn.sigmoid(
            jnp.dot(wg_t[1], normed, preferred_element_type=F32)
        )

    arrive(7, 0, t1_got)
    for q in range(4):
        square[q] = t1_got[lanes(q, 4)].astype(F32).reshape(128, 128).T
    for a in range(4):
        rows = [
            jnp.concatenate(
                [square.at[q][pl.ds(4 * a + b, 8, stride=16), :] for q in range(4)], axis=0
            )
            for b in range(4)
        ]
        for t in range(4):
            mixed = jnp.concatenate([rows[b][:, lanes(t, 32)] for b in range(4)], axis=1)
            for q in range(4):
                fan[a, lanes(4 * q + t, 8)] = mixed[lanes(q, 8)]
        for peer in range(GROUP):
            t2_send[a, peer] = fan.at[a][pl.ds(peer, 16, stride=8), :].astype(BF16)
        if a % 2:
            spread(
                8, a // 2, g_peer,
                lambda peer: t2_send.at[pl.ds(a - 1, 2), peer],
                t2_got.at[pl.ds(a - 1, 2), pl.ds(pl.multiple_of(g * 16, 16), 16), :],
            )
    for half in range(2):
        arrive(8, half, t2_got.at[pl.ds(2 * half, 2)])
        product = jnp.concatenate(
            [t2_got[2 * half + n].astype(F32) for n in range(2)], axis=1
        )
        there = lanes(half, 256)
        updated = middle_t[:, there] + home_gate[:, there] * jnp.dot(
            wf_t[1], norm0(product).astype(BF16), preferred_element_type=F32
        )
        for n in range(2):
            out_ref[lanes(2 * half + n, 4)] = updated[:, lanes(n)].T.reshape(4, 32, 128)

    leave(0, z_send.at[pl.ds(0, 14)])
    leave(1, h_send.at[:, pl.ds(0, 112), :])
    leave(4, c2_send.at[:, pl.ds(0, 14)])
    leave(5, b1_send.at[:, :, :, pl.ds(0, 112), :])
    leave(8, t2_send.at[:, pl.ds(0, 7)])
    leave(9, u_send.at[:, pl.ds(0, 224), :])

    @pl.when(is_owner)
    def _():
        leave(2, k_send.at[pl.ds(0, 15)])
        leave(3, size63)
        leave(6, b2_send.at[:, pl.ds(0, 15)])
        leave(7, size63)

    @pl.when(jnp.logical_not(is_owner))
    def _():
        leave(2, k_send)
        leave(6, b2_send)


def body(pair, out_inputs, out_gate, out_final, in_inputs, in_gate, in_final):
    anywhere = pl.BlockSpec(memory_space=pl.ANY)
    return pl.pallas_call(
        kernel,
        out_shape=jax.ShapeDtypeStruct((16, 32, 128), F32),
        in_specs=[anywhere] * 7,
        out_specs=pl.BlockSpec(memory_space=pltpu.VMEM),
        scratch_shapes=[
            pltpu.VMEM((16, 32, 128), F32),
            pltpu.VMEM((2, 128, 512), BF16),
            pltpu.VMEM((2, 128, 128), BF16),
            pltpu.VMEM((2, 128, 128), BF16),
            pltpu.VMEM((16, 32, 128), BF16),
            pltpu.VMEM((2, 256, 128), BF16),
            pltpu.VMEM((2, 512, 128), BF16),
            pltpu.VMEM((2, 128, 128), BF16),
            pltpu.VMEM((2, 128, 128), BF16),
            pltpu.VMEM((2, 128, 256), F32),
            pltpu.VMEM((2, 128, 256), F32),
            pltpu.VMEM((2, 128, 256), F32),
            pltpu.VMEM((2, 128, 512), BF16),
            pltpu.VMEM((2, 8, 16, 512), BF16),
            pltpu.VMEM((4, 128, 128), F32),
            pltpu.VMEM((4, 128, 128), F32),
            pltpu.VMEM((16, 2, 32, 128), BF16),
            pltpu.VMEM((2, 2, 2, 128, 128), BF16),
            pltpu.VMEM((2, 2, 16, 16, 128), BF16),
            pltpu.VMEM((256, 128), F32),
            pltpu.VMEM((2, 16, 2, 16, 128), BF16),
            pltpu.VMEM((2, 2, 512, 512), BF16),
            pltpu.VMEM((2, 512, 256), BF16),
            pltpu.VMEM((2, 16, 16, 128), BF16),
            pltpu.VMEM((2, 16, 16, 128), BF16),
            pltpu.VMEM((2, 2, 128, 128), BF16),
            pltpu.VMEM((512, 512), BF16),
            pltpu.VMEM((16, 32, 128), BF16),
            pltpu.VMEM((4, 8, 16, 128), BF16),
            pltpu.VMEM((4, 128, 128), BF16),
            pltpu.VMEM((2, 256, 128), BF16),
            pltpu.VMEM((16, 32, 128), BF16),
            pltpu.VMEM((128, 512), F32),
            pltpu.VMEM((128, 512), F32),
            pltpu.VMEM((512, 512), BF16),
            pltpu.VMEM((1008, 256), BF16),
            pltpu.SemaphoreType.DMA((PHASES,)),
            pltpu.SemaphoreType.DMA((PHASES, 2)),
            pltpu.SemaphoreType.DMA((7,)),
            pltpu.SemaphoreType.REGULAR,
        ],
        compiler_params=pltpu.CompilerParams(
            collective_id=0, has_side_effects=True, vmem_limit_bytes=60 * 1024 * 1024
        ),
        name="triangles",
    )(pair, out_inputs, out_gate, out_final, in_inputs, in_gate, in_final)


def solution(mesh):
    placed = (P("row", "ch", None), P(), P(), P(), P(), P(), P())
    return jax.shard_map(
        body, mesh=mesh, in_specs=placed, out_specs=P("row", "ch", None), check_vma=False
    )
```

time: 87.8 us -> 77.4 us (0.88)
  Pallas kernels: 86 us -> 75.5 us
  local copies, waits for them, and re-layouts: 0.01 us -> 1.67 us
  other arithmetic: 1.64 us -> 0 us
    pallas_call x1, Pallas kernels: 86 us -> 75.5 us  [body(): pl.pallas_call(kernel, out_shape=jax.ShapeDtypeStruct((16, 32, 128), F32)...]
    unnamed x2 -> x1, local copies, waits for them, and re-layouts: 0.01 us -> 1.67 us
    add x1 -> x0, other arithmetic: 1.64 us -> none  [body(): return pair + total.astype(F32)]
where the time goes in v3:
time: 77.4 us; the launch traced here: 77.2 us
  Pallas kernels  75.5 us (98%)
  local copies, waits for them, and re-layouts  1.67 us (2%)
    pallas_call x1, Pallas kernels, body(): pl.pallas_call(kernel, out_shape=jax.ShapeDtypeStruct((16, 32, 128), F32)...  75.5 us
    unnamed x1, local copies, waits for them, and re-layouts  1.67 us

profile of v3, /device:TPU:1, one launch (start us, length us, event | category | flops | bytes accessed | tf_op | source)
XLA Modules:
  0.0 77.2 jit_solution(17165300260317087441)
XLA Ops:
  0.0 75.5 %triangles.1 = f32[16,32,128]{2,1,0:T(8,128)} custom-call(f32[16,32,128]{2,1,0:T(8,128)} %z_hbm.1, bf16[128,512]{1,0:T(8,128)(2,1)} %wi0.1, bf16[128,128]{1,0:T(8,128)(2,1)} %wg0.1, bf16[128,128]{1,0:T(8,128)(2,1)} %wf0.1, bf16[128,512]{1,0:T(8,128)(2,1)} %wi1.1, bf16[128,128]{1,0:T(8,128)(2,1)} %wg1.1, bf16[128,128]{1,0:T(8,128)(2,1)} %wf1.1), custom_call_target="tpu_custom_call" | custom-call | tf_op jit(solution)/shard_map/triangles/pallas_call | solution.py:423
  75.6 1.7 %copy.9 = f32[16,32,128]{2,1,0:T(8,128)} copy(f32[16,32,128]{2,1,0:T(8,128)} %triangles.1) | data formatting | bytes 524288

commit v4 on v3

--- a/solution.py
+++ b/solution.py
@@ -14,6 +14,14 @@
 PHASES = 10
 
 
+def mod(a, b):
+    return lax.rem(a, jnp.int32(b))
+
+
+def div(a, b):
+    return lax.div(a, jnp.int32(b))
+
+
 def norm0(values):
     mean = jnp.mean(values, axis=0, keepdims=True)
     centered = values - mean
@@ -30,20 +38,20 @@
 
 
 def kernel(
-    z_hbm, wi0, wg0, wf0, wi1, wg1, wf1, out_ref,
+    z_hbm, wi0, wg0, wf0, wi1, wg1, wf1, out_hbm,
     z_in, wi_in, wg_in, wf_in, z_send, z_got, wi_t, wg_t, wf_t, zt, acc, gate,
     h_send, h_got, fan, square, k_send, b1_send, b1_got, turn, b2_send, operands,
     x1_send, c1_got, c2_send, c2_got, x2_send, t1_got, t2_send, t2_got,
-    u_send, u_got, middle_t, home_gate, turned, size63, send_sem, recv_sem, in_sem, ready,
+    u_send, u_got, middle_t, home_gate, result, turned, size63, send_sem, recv_sem, in_sem, out_sem, ready,
 ):
     row = lax.axis_index("row")
     ch = lax.axis_index("ch")
-    y, zhi = ch // 2, ch % 2
-    x, zlo, core = row // 8, row % 8 // 2, row % 2
+    y, zhi = div(ch, 2), mod(ch, 2)
+    x, zlo, core = div(row, 8), div(mod(row, 8), 2), mod(row, 2)
     g = x * 2 + core
 
     def owner_zlo(m):
-        return m // 2 % 2 + 2 * ((m // 4 + core) % 2)
+        return mod(div(m, 2), 2) + 2 * mod(div(m, 4) + core, 2)
 
     def plane(peer_zlo):
         return x * 8 + peer_zlo * 2 + core
@@ -67,16 +75,16 @@
         pltpu.make_async_copy(ref, ref, send_sem.at[phase]).wait()
 
     def y_peer(step):
-        peer = (y + step) % GROUP
+        peer = mod(y + step, GROUP)
         return peer, row, peer * 2 + zhi
 
     def g_peer(step):
-        peer = (g + step) % GROUP
-        return peer, peer // 2 * 8 + zlo * 2 + peer % 2, ch
+        peer = mod(g + step, GROUP)
+        return peer, div(peer, 2) * 8 + zlo * 2 + mod(peer, 2), ch
 
     def z_peer(step):
-        peer = (zhi * 4 + zlo + step) % GROUP
-        return peer, plane(peer % 4), y * 2 + peer // 4
+        peer = mod(zhi * 4 + zlo + step, GROUP)
+        return peer, plane(mod(peer, 4)), y * 2 + div(peer, 4)
 
     def spread(phase, chunk, peer_of, src_of, dst):
         for step in FAR_FIRST:
@@ -88,7 +96,7 @@
         for dy in (*FAR_FIRST, 0):
             for dz in (1, 0):
                 if dy or dz:
-                    yield (y + dy) % 8 * 2 + (zhi + dz) % 2
+                    yield mod(y + dy, 8) * 2 + mod(zhi + dz, 2)
 
     def to_owners(phase, chunk, src_of, here):
         for m in others():
@@ -208,8 +216,8 @@
         arrive(2, 1, operands.at[0, 1])
 
         def back(step, carry):
-            chunk = step // 4
-            peer_zlo = (zlo + 1 + step) % 4
+            chunk = div(step, 4)
+            peer_zlo = mod(zlo + 1 + step, 4)
             rows = pl.ds(pl.multiple_of(peer_zlo * 128, 128), 128)
             columns = pl.ds(pl.multiple_of(chunk * 256, 256), 256)
             x1_send[chunk, rows, :] = jnp.dot(
@@ -219,8 +227,8 @@
 
             def block(peer_ch):
                 return x1_send.at[
-                    chunk, pl.ds(place(peer_zlo, peer_ch // 2), 16),
-                    pl.ds(pl.multiple_of(peer_ch % 2 * 128, 128), 128),
+                    chunk, pl.ds(place(peer_zlo, div(peer_ch, 2)), 16),
+                    pl.ds(pl.multiple_of(mod(peer_ch, 2) * 128, 128), 128),
                 ]
 
             for peer_ch in others():
@@ -275,27 +283,27 @@
             )
             for i in range(2):
                 b1_send[chunk, side, i] = value[:, lanes(i)]
-        spread(
-            5, chunk, g_peer,
-            lambda peer: b1_send.at[
-                chunk, :, :, pl.ds(pl.multiple_of(peer * 16, 16), 16), :
-            ],
-            b1_got.at[chunk, :, pl.ds(g * 2, 2)],
-        )
+            spread(
+                5, chunk * 2 + side, g_peer,
+                lambda peer: b1_send.at[
+                    chunk, side, :, pl.ds(pl.multiple_of(peer * 16, 16), 16), :
+                ],
+                b1_got.at[chunk, side, pl.ds(g * 2, 2)],
+            )
 
     both(middle)
 
     def second_to_owners(chunk):
-        arrive(5, chunk, b1_got.at[chunk])
         for side in range(2):
-            swap(b1_got.at[chunk, side], lambda c: b2_send.at[chunk, c, side])
-        to_owners(
-            6, chunk, lambda m: b2_send.at[chunk, m],
-            operands.at[
-                1, :, pl.ds(place(zlo, y), 16),
-                pl.ds(pl.multiple_of(chunk * 256 + zhi * 128, 128), 128),
-            ],
-        )
+            arrive(5, chunk * 2 + side, b1_got.at[chunk, side])
+            swap(b1_got.at[chunk, side], lambda c: b2_send.at[chunk, side, c])
+            to_owners(
+                6, chunk, lambda m: b2_send.at[chunk, side, m],
+                operands.at[
+                    1, side, pl.ds(place(zlo, y), 16),
+                    pl.ds(pl.multiple_of(chunk * 256 + zhi * 128, 128), 128),
+                ],
+            )
 
     both(second_to_owners)
 
@@ -316,106 +324,117 @@
             arrive(6, chunk, operands.at[1, :, :, pl.ds(chunk * 256, 256)])
             for q in (2 * chunk, 2 * chunk + 1):
                 turned[lanes(q), :] = operands[1, 1, :, lanes(q)].T
-        mine = t1_got.at[ch]
-        own = y % 2 * 2 + zhi
+        own = mod(y, 2) * 2 + zhi
 
         def back(step, carry):
-            part = (own + 1 + step) % 4
+            part, half = mod(own + 1 + step, 4), div(step, 4)
             rows = pl.ds(pl.multiple_of(part * 128, 128), 128)
-            x2_send[rows, :] = jnp.dot(
-                turned[rows, :], operands[1, 0], preferred_element_type=F32
-            ).astype(BF16)
+
+            @pl.when(half == 0)
+            def _():
+                x2_send[rows, :] = jnp.dot(
+                    turned[rows, :], operands[1, 0], preferred_element_type=F32
+                ).astype(BF16)
+
+            mine = t1_got.at[half, ch]
 
             def go(peer_zlo, k, is_self=False):
                 src = x2_send.at[
-                    pl.ds(pl.multiple_of(part * 128 + k * 32, 32), 32),
+                    pl.ds(pl.multiple_of(part * 128 + k * 32 + half * 16, 16), 16),
                     pl.ds(pl.multiple_of(peer_zlo * 128, 128), 128),
                 ]
                 if is_self:
-                    keep(7, 0, src, mine)
+                    keep(7, half, src, mine)
                 else:
-                    send(7, 0, src, mine, plane(peer_zlo),
-                         (2 * k + part // 2) * 2 + part % 2)
+                    send(7, half, src, mine, plane(peer_zlo),
+                         (2 * k + div(part, 2)) * 2 + mod(part, 2))
 
             for dk in (2, 1, 3, 0):
                 for dz in (2, 1, 3, 0):
                     if dk or dz:
-                        go((zlo + dz) % 4, (y // 2 + dk) % 4)
+                        go(mod(zlo + dz, 4), mod(div(y, 2) + dk, 4))
 
             @pl.when(part == own)
             def _():
-                go(zlo, y // 2, True)
+                go(zlo, div(y, 2), True)
 
             @pl.when(part != own)
             def _():
-                go(zlo, y // 2)
+                go(zlo, div(y, 2))
 
             return carry
 
-        lax.fori_loop(0, 4, back, 0)
+        lax.fori_loop(0, 8, back, 0)
 
     arrive(9, 0, u_got)
-    for a in range(4):
-        block = z_in[lanes(a, 4)] + u_got[lanes(a, 4)].astype(F32)
-        middle_t[:, lanes(a)] = block.reshape(128, 128).T
     for half in range(2):
-        normed = norm0(middle_t[:, lanes(half, 256)]).astype(BF16)
-        home_gate[:, lanes(half, 256)] = jax.nn.sigmoid(
-            jnp.dot(wg_t[1], normed, preferred_element_type=F32)
-        )
-
-    arrive(7, 0, t1_got)
-    for q in range(4):
-        square[q] = t1_got[lanes(q, 4)].astype(F32).reshape(128, 128).T
-    for a in range(4):
-        rows = [
-            jnp.concatenate(
-                [square.at[q][pl.ds(4 * a + b, 8, stride=16), :] for q in range(4)], axis=0
+        block = z_in[:, lanes(half, 16)] + u_got[:, lanes(half, 16)].astype(F32)
+        middle_t[half] = block.reshape(256, 128).T
+        home_gate[half] = jax.nn.sigmoid(
+            jnp.dot(
+                wg_t[1], norm0(middle_t[half]).astype(BF16), preferred_element_type=F32
             )
-            for b in range(4)
-        ]
-        for t in range(4):
-            mixed = jnp.concatenate([rows[b][:, lanes(t, 32)] for b in range(4)], axis=1)
-            for q in range(4):
-                fan[a, lanes(4 * q + t, 8)] = mixed[lanes(q, 8)]
-        for peer in range(GROUP):
-            t2_send[a, peer] = fan.at[a][pl.ds(peer, 16, stride=8), :].astype(BF16)
-        if a % 2:
-            spread(
-                8, a // 2, g_peer,
-                lambda peer: t2_send.at[pl.ds(a - 1, 2), peer],
-                t2_got.at[pl.ds(a - 1, 2), pl.ds(pl.multiple_of(g * 16, 16), 16), :],
-            )
+        )
+
     for half in range(2):
-        arrive(8, half, t2_got.at[pl.ds(2 * half, 2)])
-        product = jnp.concatenate(
-            [t2_got[2 * half + n].astype(F32) for n in range(2)], axis=1
-        )
-        there = lanes(half, 256)
-        updated = middle_t[:, there] + home_gate[:, there] * jnp.dot(
+        arrive(7, half, t1_got.at[half])
+        for q in range(2):
+            square[q] = t1_got[half, lanes(q, 8)].astype(F32).reshape(128, 128).T
+        for a in range(2):
+            rows = [
+                jnp.concatenate(
+                    [square.at[q][pl.ds(8 * a + b, 8, stride=16), :] for q in range(2)],
+                    axis=0,
+                )
+                for b in range(8)
+            ]
+            for t in range(8):
+                mixed = jnp.concatenate([r[:, lanes(t, 16)] for r in rows], axis=1)
+                for q in range(2):
+                    fan[a, lanes(8 * q + t, 8)] = mixed[lanes(q, 8)]
+            for peer in range(GROUP):
+                t2_send[half, a, peer] = fan.at[a][pl.ds(peer, 16, stride=8), :].astype(BF16)
+        spread(
+            8, half, g_peer,
+            lambda peer: t2_send.at[half, :, peer],
+            t2_got.at[half, :, pl.ds(pl.multiple_of(g * 16, 16), 16), :],
+        )
+    stores = []
+    for half in range(2):
+        arrive(8, half, t2_got.at[half])
+        product = jnp.concatenate([t2_got[half, a].astype(F32) for a in range(2)], axis=1)
+        updated = middle_t[half] + home_gate[half] * jnp.dot(
             wf_t[1], norm0(product).astype(BF16), preferred_element_type=F32
         )
-        for n in range(2):
-            out_ref[lanes(2 * half + n, 4)] = updated[:, lanes(n)].T.reshape(4, 32, 128)
+        there = pl.ds(half * 16, 16)
+        result[:, there] = updated.T.reshape(16, 16, 128)
+        store = pltpu.make_async_copy(
+            result.at[:, there], out_hbm.at[:, there], out_sem.at[half]
+        )
+        store.start()
+        stores.append(store)
 
     leave(0, z_send.at[pl.ds(0, 14)])
     leave(1, h_send.at[:, pl.ds(0, 112), :])
     leave(4, c2_send.at[:, pl.ds(0, 14)])
     leave(5, b1_send.at[:, :, :, pl.ds(0, 112), :])
-    leave(8, t2_send.at[:, pl.ds(0, 7)])
+    leave(8, t2_send.at[:, :, pl.ds(0, 7)])
     leave(9, u_send.at[:, pl.ds(0, 224), :])
 
     @pl.when(is_owner)
     def _():
         leave(2, k_send.at[pl.ds(0, 15)])
         leave(3, size63)
-        leave(6, b2_send.at[:, pl.ds(0, 15)])
+        leave(6, b2_send.at[:, :, pl.ds(0, 15)])
         leave(7, size63)
 
     @pl.when(jnp.logical_not(is_owner))
     def _():
         leave(2, k_send)
         leave(6, b2_send)
+
+    for store in stores:
+        store.wait()
 
 
 def body(pair, out_inputs, out_gate, out_final, in_inputs, in_gate, in_final):
@@ -424,7 +443,7 @@
         kernel,
         out_shape=jax.ShapeDtypeStruct((16, 32, 128), F32),
         in_specs=[anywhere] * 7,
-        out_specs=pl.BlockSpec(memory_space=pltpu.VMEM),
+        out_specs=anywhere,
         scratch_shapes=[
             pltpu.VMEM((16, 32, 128), F32),
             pltpu.VMEM((2, 128, 512), BF16),
@@ -446,25 +465,27 @@
             pltpu.VMEM((2, 2, 2, 128, 128), BF16),
             pltpu.VMEM((2, 2, 16, 16, 128), BF16),
             pltpu.VMEM((256, 128), F32),
-            pltpu.VMEM((2, 16, 2, 16, 128), BF16),
+            pltpu.VMEM((2, 2, 16, 16, 128), BF16),
             pltpu.VMEM((2, 2, 512, 512), BF16),
             pltpu.VMEM((2, 512, 256), BF16),
             pltpu.VMEM((2, 16, 16, 128), BF16),
             pltpu.VMEM((2, 16, 16, 128), BF16),
             pltpu.VMEM((2, 2, 128, 128), BF16),
             pltpu.VMEM((512, 512), BF16),
-            pltpu.VMEM((16, 32, 128), BF16),
-            pltpu.VMEM((4, 8, 16, 128), BF16),
-            pltpu.VMEM((4, 128, 128), BF16),
+            pltpu.VMEM((2, 16, 16, 128), BF16),
+            pltpu.VMEM((2, 2, 8, 16, 128), BF16),
+            pltpu.VMEM((2, 2, 128, 128), BF16),
             pltpu.VMEM((2, 256, 128), BF16),
             pltpu.VMEM((16, 32, 128), BF16),
-            pltpu.VMEM((128, 512), F32),
-            pltpu.VMEM((128, 512), F32),
+            pltpu.VMEM((2, 128, 256), F32),
+            pltpu.VMEM((2, 128, 256), F32),
+            pltpu.VMEM((16, 32, 128), F32),
             pltpu.VMEM((512, 512), BF16),
             pltpu.VMEM((1008, 256), BF16),
             pltpu.SemaphoreType.DMA((PHASES,)),
-            pltpu.SemaphoreType.DMA((PHASES, 2)),
+            pltpu.SemaphoreType.DMA((PHASES, 4)),
             pltpu.SemaphoreType.DMA((7,)),
+            pltpu.SemaphoreType.DMA((2,)),
             pltpu.SemaphoreType.REGULAR,
         ],
         compiler_params=pltpu.CompilerParams(

time: 77.4 us -> 77.7 us (level)
  no operation moved by 1% of the time
where the time goes in v4:
time: 77.7 us; the launch traced here: 77.5 us
  Pallas kernels  75.8 us (98%)
  local copies, waits for them, and re-layouts  1.67 us (2%)
    pallas_call x1, Pallas kernels, body(): pl.pallas_call(kernel, out_shape=jax.ShapeDtypeStruct((16, 32, 128), F32)...  75.8 us
    unnamed x1, local copies, waits for them, and re-layouts  1.67 us

profile of v4, /device:TPU:1, one launch (start us, length us, event | category | flops | bytes accessed | tf_op | source)
XLA Modules:
  0.0 77.5 jit_solution(12847359599673718231)
XLA Ops:
  0.0 75.8 %triangles.1 = f32[16,32,128]{2,1,0:T(8,128)} custom-call(f32[16,32,128]{2,1,0:T(8,128)} %z_hbm.1, bf16[128,512]{1,0:T(8,128)(2,1)} %wi0.1, bf16[128,128]{1,0:T(8,128)(2,1)} %wg0.1, bf16[128,128]{1,0:T(8,128)(2,1)} %wf0.1, bf16[128,512]{1,0:T(8,128)(2,1)} %wi1.1, bf16[128,128]{1,0:T(8,128)(2,1)} %wg1.1, bf16[128,128]{1,0:T(8,128)(2,1)} %wf1.1), custom_call_target="tpu_custom_call" | custom-call | tf_op jit(solution)/shard_map/triangles/pallas_call | solution.py:442
  75.8 1.7 %copy.9 = f32[16,32,128]{2,1,0:T(8,128)} copy(f32[16,32,128]{2,1,0:T(8,128)} %triangles.1) | data formatting | bytes 524288

commit v5 on v3

--- a/solution.py
+++ b/solution.py
@@ -11,7 +11,15 @@
 GROUP = 8
 OWNERS = 16
 FAR_FIRST = (4, 3, 5, 2, 6, 1, 7)
-PHASES = 10
+PHASES = 12
+
+
+def mod(a, b):
+    return lax.rem(a, jnp.int32(b))
+
+
+def div(a, b):
+    return lax.div(a, jnp.int32(b))
 
 
 def norm0(values):
@@ -30,25 +38,27 @@
 
 
 def kernel(
-    z_hbm, wi0, wg0, wf0, wi1, wg1, wf1, out_ref,
+    z_hbm, wi0, wg0, wf0, wi1, wg1, wf1, out_hbm,
     z_in, wi_in, wg_in, wf_in, z_send, z_got, wi_t, wg_t, wf_t, zt, acc, gate,
     h_send, h_got, fan, square, k_send, b1_send, b1_got, turn, b2_send, operands,
     x1_send, c1_got, c2_send, c2_got, x2_send, t1_got, t2_send, t2_got,
-    u_send, u_got, middle_t, home_gate, turned, size63, send_sem, recv_sem, in_sem, ready,
+    u_send, u_got, middle_t, home_gate, result, turned, size63, send_sem, recv_sem, in_sem, out_sem, ready,
 ):
     row = lax.axis_index("row")
     ch = lax.axis_index("ch")
-    y, zhi = ch // 2, ch % 2
-    x, zlo, core = row // 8, row % 8 // 2, row % 2
+    y, zhi = div(ch, 2), mod(ch, 2)
+    x, zlo, core = div(row, 8), div(mod(row, 8), 2), mod(row, 2)
     g = x * 2 + core
 
-    def owner_zlo(m):
-        return m // 2 % 2 + 2 * ((m // 4 + core) % 2)
-
-    def plane(peer_zlo):
-        return x * 8 + peer_zlo * 2 + core
-
+    def owner_zlo(m, of_core=core):
+        return mod(div(m, 2), 2) + 2 * mod(div(m, 4) + of_core, 2)
+
+    def plane(peer_zlo, of_core=core):
+        return x * 8 + peer_zlo * 2 + of_core
+
+    other_core = 1 - core
     is_owner = zlo == owner_zlo(ch)
+    is_mate = zlo == owner_zlo(ch, other_core)
 
     def send(phase, chunk, src, dst, to_row, to_ch):
         pltpu.make_async_remote_copy(
@@ -67,16 +77,16 @@
         pltpu.make_async_copy(ref, ref, send_sem.at[phase]).wait()
 
     def y_peer(step):
-        peer = (y + step) % GROUP
+        peer = mod(y + step, GROUP)
         return peer, row, peer * 2 + zhi
 
     def g_peer(step):
-        peer = (g + step) % GROUP
-        return peer, peer // 2 * 8 + zlo * 2 + peer % 2, ch
+        peer = mod(g + step, GROUP)
+        return peer, div(peer, 2) * 8 + zlo * 2 + mod(peer, 2), ch
 
     def z_peer(step):
-        peer = (zhi * 4 + zlo + step) % GROUP
-        return peer, plane(peer % 4), y * 2 + peer // 4
+        peer = mod(zhi * 4 + zlo + step, GROUP)
+        return peer, plane(mod(peer, 4)), y * 2 + div(peer, 4)
 
     def spread(phase, chunk, peer_of, src_of, dst):
         for step in FAR_FIRST:
@@ -88,7 +98,7 @@
         for dy in (*FAR_FIRST, 0):
             for dz in (1, 0):
                 if dy or dz:
-                    yield (y + dy) % 8 * 2 + (zhi + dz) % 2
+                    yield mod(y + dy, 8) * 2 + mod(zhi + dz, 2)
 
     def to_owners(phase, chunk, src_of, here):
         for m in others():
@@ -200,6 +210,16 @@
         wg_t[u] = flip(wg_in[u])
         wf_t[u] = flip(wf_in[u])
 
+    def part_of(step):
+        peer_zlo = mod(zlo + 1 + step, 4)
+        return peer_zlo, pl.ds(pl.multiple_of(peer_zlo * 128, 128), 128)
+
+    def block(chunk, peer_zlo, peer_ch):
+        return x1_send.at[
+            chunk, pl.ds(place(peer_zlo, div(peer_ch, 2)), 16),
+            pl.ds(pl.multiple_of(mod(peer_ch, 2) * 128, 128), 128),
+        ]
+
     @pl.when(is_owner)
     def _():
         arrive(2, 0, operands.at[0, 0])
@@ -207,36 +227,43 @@
             turned[lanes(q), :] = operands[0, 0, :, lanes(q)].T
         arrive(2, 1, operands.at[0, 1])
 
+        mine = c1_got.at[0, ch]
+
         def back(step, carry):
-            chunk = step // 4
-            peer_zlo = (zlo + 1 + step) % 4
-            rows = pl.ds(pl.multiple_of(peer_zlo * 128, 128), 128)
-            columns = pl.ds(pl.multiple_of(chunk * 256, 256), 256)
-            x1_send[chunk, rows, :] = jnp.dot(
-                turned[rows, :], operands[0, 1, :, columns], preferred_element_type=F32
+            peer_zlo, rows = part_of(step)
+            product = jnp.dot(
+                turned[rows, :], operands[0, 1], preferred_element_type=F32
             ).astype(BF16)
-            mine = c1_got.at[chunk, ch]
-
-            def block(peer_ch):
-                return x1_send.at[
-                    chunk, pl.ds(place(peer_zlo, peer_ch // 2), 16),
-                    pl.ds(pl.multiple_of(peer_ch % 2 * 128, 128), 128),
-                ]
-
+            x1_send[1, rows, :] = product[:, 256:]
+            there = x1_send.at[1, rows, :]
+            send(10, step, there, there, plane(zlo, other_core), ch)
+            x1_send[0, rows, :] = product[:, :256]
             for peer_ch in others():
-                send(3, chunk, block(peer_ch), mine, plane(peer_zlo), peer_ch)
+                send(3, 0, block(0, peer_zlo, peer_ch), mine, plane(peer_zlo), peer_ch)
 
             @pl.when(peer_zlo == zlo)
             def _():
-                keep(3, chunk, block(ch), mine)
+                keep(3, 0, block(0, peer_zlo, ch), mine)
 
             @pl.when(peer_zlo != zlo)
             def _():
-                send(3, chunk, block(ch), mine, plane(peer_zlo), ch)
+                send(3, 0, block(0, peer_zlo, ch), mine, plane(peer_zlo), ch)
 
             return carry
 
-        lax.fori_loop(0, 8, back, 0)
+        lax.fori_loop(0, 4, back, 0)
+
+    @pl.when(is_mate)
+    def _():
+        def back(step, carry):
+            peer_zlo, rows = part_of(step)
+            arrive(10, step, x1_send.at[1, rows, :])
+            for peer_ch in (*others(), ch):
+                send(3, 1, block(1, peer_zlo, peer_ch), c1_got.at[1, ch],
+                     plane(peer_zlo, other_core), peer_ch)
+            return carry
+
+        lax.fori_loop(0, 4, back, 0)
 
     arrive(0, 0, z_got)
     for chunk in range(2):
@@ -310,49 +337,54 @@
         u_got.at[pl.ds(y * 2, 2)],
     )
 
+    own = mod(y, 2) * 2 + zhi
+
+    def columns_part(step):
+        part = mod(own + 1 + step, 4)
+        return part, pl.ds(pl.multiple_of(part * 128, 128), 128)
+
+    def piece(part, peer_zlo, k):
+        return x2_send.at[
+            pl.ds(pl.multiple_of(part * 128 + k * 32, 32), 32),
+            pl.ds(pl.multiple_of(peer_zlo * 128, 128), 128),
+        ]
+
+    def go(part, of_core, with_self=True):
+        for dk in (2, 1, 3, 0):
+            for dz in (2, 1, 3, 0):
+                if dk or dz or with_self:
+                    peer_zlo, k = mod(zlo + dz, 4), mod(div(y, 2) + dk, 4)
+                    send(7, 0, piece(part, peer_zlo, k), t1_got.at[ch],
+                         plane(peer_zlo, of_core), (2 * k + div(part, 2)) * 2 + mod(part, 2))
+
     @pl.when(is_owner)
     def _():
         for chunk in range(2):
             arrive(6, chunk, operands.at[1, :, :, pl.ds(chunk * 256, 256)])
             for q in (2 * chunk, 2 * chunk + 1):
                 turned[lanes(q), :] = operands[1, 1, :, lanes(q)].T
-        mine = t1_got.at[ch]
-        own = y % 2 * 2 + zhi
-
-        def back(step, carry):
-            part = (own + 1 + step) % 4
-            rows = pl.ds(pl.multiple_of(part * 128, 128), 128)
+
+        def multiply(rows):
             x2_send[rows, :] = jnp.dot(
                 turned[rows, :], operands[1, 0], preferred_element_type=F32
             ).astype(BF16)
 
-            def go(peer_zlo, k, is_self=False):
-                src = x2_send.at[
-                    pl.ds(pl.multiple_of(part * 128 + k * 32, 32), 32),
-                    pl.ds(pl.multiple_of(peer_zlo * 128, 128), 128),
-                ]
-                if is_self:
-                    keep(7, 0, src, mine)
-                else:
-                    send(7, 0, src, mine, plane(peer_zlo),
-                         (2 * k + part // 2) * 2 + part % 2)
-
-            for dk in (2, 1, 3, 0):
-                for dz in (2, 1, 3, 0):
-                    if dk or dz:
-                        go((zlo + dz) % 4, (y // 2 + dk) % 4)
-
-            @pl.when(part == own)
-            def _():
-                go(zlo, y // 2, True)
-
-            @pl.when(part != own)
-            def _():
-                go(zlo, y // 2)
-
-            return carry
-
-        lax.fori_loop(0, 4, back, 0)
+        for step in range(0, 4, 2):
+            part, rows = columns_part(step)
+            multiply(rows)
+            there = x2_send.at[rows, :]
+            send(11, step, there, there, plane(zlo, other_core), ch)
+            part, rows = columns_part(step + 1)
+            multiply(rows)
+            go(part, core, with_self=step == 0)
+        keep(7, 0, piece(own, zlo, div(y, 2)), t1_got.at[ch])
+
+    @pl.when(is_mate)
+    def _():
+        for step in range(0, 4, 2):
+            part, rows = columns_part(step)
+            arrive(11, step, x2_send.at[rows, :])
+            go(part, other_core)
 
     arrive(9, 0, u_got)
     for a in range(4):
@@ -386,6 +418,7 @@
                 lambda peer: t2_send.at[pl.ds(a - 1, 2), peer],
                 t2_got.at[pl.ds(a - 1, 2), pl.ds(pl.multiple_of(g * 16, 16), 16), :],
             )
+    stores = []
     for half in range(2):
         arrive(8, half, t2_got.at[pl.ds(2 * half, 2)])
         product = jnp.concatenate(
@@ -395,8 +428,11 @@
         updated = middle_t[:, there] + home_gate[:, there] * jnp.dot(
             wf_t[1], norm0(product).astype(BF16), preferred_element_type=F32
         )
-        for n in range(2):
-            out_ref[lanes(2 * half + n, 4)] = updated[:, lanes(n)].T.reshape(4, 32, 128)
+        home = pl.ds(half * 8, 8)
+        result[home] = updated.T.reshape(8, 32, 128)
+        store = pltpu.make_async_copy(result.at[home], out_hbm.at[home], out_sem.at[half])
+        store.start()
+        stores.append(store)
 
     leave(0, z_send.at[pl.ds(0, 14)])
     leave(1, h_send.at[:, pl.ds(0, 112), :])
@@ -410,12 +446,22 @@
         leave(2, k_send.at[pl.ds(0, 15)])
         leave(3, size63)
         leave(6, b2_send.at[:, pl.ds(0, 15)])
-        leave(7, size63)
+        leave(7, size63.at[pl.ds(0, 992)])
+        leave(10, x1_send.at[1])
+        leave(11, x2_send.at[pl.ds(0, 256)])
 
     @pl.when(jnp.logical_not(is_owner))
     def _():
         leave(2, k_send)
         leave(6, b2_send)
+
+    @pl.when(is_mate)
+    def _():
+        leave(3, x1_send.at[1])
+        leave(7, x2_send.at[pl.ds(0, 256)])
+
+    for store in stores:
+        store.wait()
 
 
 def body(pair, out_inputs, out_gate, out_final, in_inputs, in_gate, in_final):
@@ -424,7 +470,7 @@
         kernel,
         out_shape=jax.ShapeDtypeStruct((16, 32, 128), F32),
         in_specs=[anywhere] * 7,
-        out_specs=pl.BlockSpec(memory_space=pltpu.VMEM),
+        out_specs=anywhere,
         scratch_shapes=[
             pltpu.VMEM((16, 32, 128), F32),
             pltpu.VMEM((2, 128, 512), BF16),
@@ -460,11 +506,13 @@
             pltpu.VMEM((16, 32, 128), BF16),
             pltpu.VMEM((128, 512), F32),
             pltpu.VMEM((128, 512), F32),
+            pltpu.VMEM((16, 32, 128), F32),
             pltpu.VMEM((512, 512), BF16),
-            pltpu.VMEM((1008, 256), BF16),
+            pltpu.VMEM((1008, 128), BF16),
             pltpu.SemaphoreType.DMA((PHASES,)),
-            pltpu.SemaphoreType.DMA((PHASES, 2)),
+            pltpu.SemaphoreType.DMA((PHASES, 4)),
             pltpu.SemaphoreType.DMA((7,)),
+            pltpu.SemaphoreType.DMA((2,)),
             pltpu.SemaphoreType.REGULAR,
         ],
         compiler_params=pltpu.CompilerParams(

time: 77.4 us -> 79.9 us (1.032)
  Pallas kernels: 75.5 us -> 78.1 us
    pallas_call x1, Pallas kernels: 75.5 us -> 78.1 us  [body(): pl.pallas_call(kernel, out_shape=jax.ShapeDtypeStruct((16, 32, 128), F32)...]
where the time goes in v5:
time: 79.9 us; the launch traced here: 79.8 us
  Pallas kernels  78.1 us (98%)
  local copies, waits for them, and re-layouts  1.67 us (2%)
    pallas_call x1, Pallas kernels, body(): pl.pallas_call(kernel, out_shape=jax.ShapeDtypeStruct((16, 32, 128), F32)...  78.1 us
    unnamed x1, local copies, waits for them, and re-layouts  1.67 us

profile of v5, /device:TPU:1, one launch (start us, length us, event | category | flops | bytes accessed | tf_op | source)
XLA Modules:
  0.0 79.8 jit_solution(10385119308951735596)
XLA Ops:
  0.0 78.1 %triangles.1 = f32[16,32,128]{2,1,0:T(8,128)} custom-call(f32[16,32,128]{2,1,0:T(8,128)} %z_hbm.1, bf16[128,512]{1,0:T(8,128)(2,1)} %wi0.1, bf16[128,128]{1,0:T(8,128)(2,1)} %wg0.1, bf16[128,128]{1,0:T(8,128)(2,1)} %wf0.1, bf16[128,512]{1,0:T(8,128)(2,1)} %wi1.1, bf16[128,128]{1,0:T(8,128)(2,1)} %wg1.1, bf16[128,128]{1,0:T(8,128)(2,1)} %wf1.1), custom_call_target="tpu_custom_call" | custom-call | tf_op jit(solution)/shard_map/triangles/pallas_call | solution.py:469
  78.1 1.7 %copy.9 = f32[16,32,128]{2,1,0:T(8,128)} copy(f32[16,32,128]{2,1,0:T(8,128)} %triangles.1) | data formatting | bytes 524288

commit v6 on v3

--- a/solution.py
+++ b/solution.py
@@ -207,36 +207,37 @@
             turned[lanes(q), :] = operands[0, 0, :, lanes(q)].T
         arrive(2, 1, operands.at[0, 1])
 
+        mine = c1_got.at[:, ch]
+
         def back(step, carry):
-            chunk = step // 4
             peer_zlo = (zlo + 1 + step) % 4
             rows = pl.ds(pl.multiple_of(peer_zlo * 128, 128), 128)
-            columns = pl.ds(pl.multiple_of(chunk * 256, 256), 256)
-            x1_send[chunk, rows, :] = jnp.dot(
-                turned[rows, :], operands[0, 1, :, columns], preferred_element_type=F32
+            product = jnp.dot(
+                turned[rows, :], operands[0, 1], preferred_element_type=F32
             ).astype(BF16)
-            mine = c1_got.at[chunk, ch]
+            for chunk in range(2):
+                x1_send[chunk, rows, :] = product[:, lanes(chunk, 256)]
 
             def block(peer_ch):
                 return x1_send.at[
-                    chunk, pl.ds(place(peer_zlo, peer_ch // 2), 16),
+                    :, pl.ds(place(peer_zlo, peer_ch // 2), 16),
                     pl.ds(pl.multiple_of(peer_ch % 2 * 128, 128), 128),
                 ]
 
             for peer_ch in others():
-                send(3, chunk, block(peer_ch), mine, plane(peer_zlo), peer_ch)
+                send(3, 0, block(peer_ch), mine, plane(peer_zlo), peer_ch)
 
             @pl.when(peer_zlo == zlo)
             def _():
-                keep(3, chunk, block(ch), mine)
+                keep(3, 0, block(ch), mine)
 
             @pl.when(peer_zlo != zlo)
             def _():
-                send(3, chunk, block(ch), mine, plane(peer_zlo), ch)
+                send(3, 0, block(ch), mine, plane(peer_zlo), ch)
 
             return carry
 
-        lax.fori_loop(0, 8, back, 0)
+        lax.fori_loop(0, 4, back, 0)
 
     arrive(0, 0, z_got)
     for chunk in range(2):
@@ -249,8 +250,9 @@
             jnp.dot(wg_t[0], norm0(zt[chunk]).astype(BF16), preferred_element_type=F32)
         )
 
+    arrive(3, 0, c1_got)
+
     def regroup(chunk):
-        arrive(3, chunk, c1_got.at[chunk])
         swap(c1_got.at[chunk], lambda i: c2_send.at[chunk, i])
         spread(
             4, chunk, g_peer,

time: 77.4 us -> 79.3 us (1.025)
  Pallas kernels: 75.5 us -> 77.4 us
    pallas_call x1, Pallas kernels: 75.5 us -> 77.4 us  [body(): pl.pallas_call(kernel, out_shape=jax.ShapeDtypeStruct((16, 32, 128), F32)...]
where the time goes in v6:
time: 79.3 us; the launch traced here: 79.1 us
  Pallas kernels  77.4 us (98%)
  local copies, waits for them, and re-layouts  1.67 us (2%)
    pallas_call x1, Pallas kernels, body(): pl.pallas_call(kernel, out_shape=jax.ShapeDtypeStruct((16, 32, 128), F32)...  77.4 us
    unnamed x1, local copies, waits for them, and re-layouts  1.67 us

profile of v6, /device:TPU:1, one launch (start us, length us, event | category | flops | bytes accessed | tf_op | source)
XLA Modules:
  0.0 79.1 jit_solution(9598607625451561607)
XLA Ops:
  0.0 77.4 %triangles.1 = f32[16,32,128]{2,1,0:T(8,128)} custom-call(f32[16,32,128]{2,1,0:T(8,128)} %z_hbm.1, bf16[128,512]{1,0:T(8,128)(2,1)} %wi0.1, bf16[128,128]{1,0:T(8,128)(2,1)} %wg0.1, bf16[128,128]{1,0:T(8,128)(2,1)} %wf0.1, bf16[128,512]{1,0:T(8,128)(2,1)} %wi1.1, bf16[128,128]{1,0:T(8,128)(2,1)} %wg1.1, bf16[128,128]{1,0:T(8,128)(2,1)} %wf1.1), custom_call_target="tpu_custom_call" | custom-call | tf_op jit(solution)/shard_map/triangles/pallas_call | solution.py:425
  77.4 1.7 %copy.9 = f32[16,32,128]{2,1,0:T(8,128)} copy(f32[16,32,128]{2,1,0:T(8,128)} %triangles.1) | data formatting | bytes 524288

commit v7 on v3

--- a/solution.py
+++ b/solution.py
@@ -159,6 +159,12 @@
             lambda peer: h_send.at[side, pl.ds(pl.multiple_of(peer * 16, 16), 16), :],
             h_got.at[side, g],
         )
+    z_send[...] = z_in[...].astype(BF16)
+    spread(
+        0, 0, y_peer,
+        lambda peer: z_send.at[pl.ds(peer * 2, 2)],
+        z_got.at[:, pl.ds(pl.multiple_of(y * 32, 32), 32), :],
+    )
     pl.semaphore_wait(ready, GROUP - 1)
 
     for side in range(2):
@@ -187,18 +193,23 @@
             ],
         )
 
-    z_send[...] = z_in[...].astype(BF16)
-    spread(
-        0, 0, y_peer,
-        lambda peer: z_send.at[pl.ds(peer * 2, 2)],
-        z_got.at[:, pl.ds(pl.multiple_of(y * 32, 32), 32), :],
-    )
     for load in loads[2:]:
         load.wait()
     wi_t[1] = flip(wi_in[1])
     for u in range(2):
         wg_t[u] = flip(wg_in[u])
         wf_t[u] = flip(wf_in[u])
+
+    arrive(0, 0, z_got)
+    for chunk in range(2):
+        for i in range(2):
+            zt[chunk, :, lanes(i)] = jnp.concatenate(
+                [z_got[i, lanes(part, 32), :].astype(F32) for part in range(chunk, 8, 2)],
+                axis=0,
+            ).T
+        gate[chunk] = jax.nn.sigmoid(
+            jnp.dot(wg_t[0], norm0(zt[chunk]).astype(BF16), preferred_element_type=F32)
+        )
 
     @pl.when(is_owner)
     def _():
@@ -237,17 +248,6 @@
             return carry
 
         lax.fori_loop(0, 8, back, 0)
-
-    arrive(0, 0, z_got)
-    for chunk in range(2):
-        for i in range(2):
-            zt[chunk, :, lanes(i)] = jnp.concatenate(
-                [z_got[i, lanes(part, 32), :].astype(F32) for part in range(chunk, 8, 2)],
-                axis=0,
-            ).T
-        gate[chunk] = jax.nn.sigmoid(
-            jnp.dot(wg_t[0], norm0(zt[chunk]).astype(BF16), preferred_element_type=F32)
-        )
 
     def regroup(chunk):
         arrive(3, chunk, c1_got.at[chunk])
@@ -317,13 +317,15 @@
             for q in (2 * chunk, 2 * chunk + 1):
                 turned[lanes(q), :] = operands[1, 1, :, lanes(q)].T
         mine = t1_got.at[ch]
-        own = y % 2 * 2 + zhi
+        own = (y % 2 * 2 + zhi) * 2 + zlo // 2
 
         def back(step, carry):
-            part = (own + 1 + step) % 4
+            place_of = (own + 1 + step) % 8
+            part, side = place_of // 2, place_of % 2
             rows = pl.ds(pl.multiple_of(part * 128, 128), 128)
-            x2_send[rows, :] = jnp.dot(
-                turned[rows, :], operands[1, 0], preferred_element_type=F32
+            columns = pl.ds(pl.multiple_of(side * 256, 256), 256)
+            x2_send[rows, columns] = jnp.dot(
+                turned[rows, :], operands[1, 0, :, columns], preferred_element_type=F32
             ).astype(BF16)
 
             def go(peer_zlo, k, is_self=False):
@@ -338,31 +340,21 @@
                          (2 * k + part // 2) * 2 + part % 2)
 
             for dk in (2, 1, 3, 0):
-                for dz in (2, 1, 3, 0):
+                for dz in (1, 0):
                     if dk or dz:
-                        go((zlo + dz) % 4, (y // 2 + dk) % 4)
-
-            @pl.when(part == own)
+                        go(side * 2 + (zlo + dz) % 2, (y // 2 + dk) % 4)
+
+            @pl.when(place_of == own)
             def _():
                 go(zlo, y // 2, True)
 
-            @pl.when(part != own)
+            @pl.when(place_of != own)
             def _():
-                go(zlo, y // 2)
+                go(side * 2 + zlo % 2, y // 2)
 
             return carry
 
-        lax.fori_loop(0, 4, back, 0)
-
-    arrive(9, 0, u_got)
-    for a in range(4):
-        block = z_in[lanes(a, 4)] + u_got[lanes(a, 4)].astype(F32)
-        middle_t[:, lanes(a)] = block.reshape(128, 128).T
-    for half in range(2):
-        normed = norm0(middle_t[:, lanes(half, 256)]).astype(BF16)
-        home_gate[:, lanes(half, 256)] = jax.nn.sigmoid(
-            jnp.dot(wg_t[1], normed, preferred_element_type=F32)
-        )
+        lax.fori_loop(0, 8, back, 0)
 
     arrive(7, 0, t1_got)
     for q in range(4):
@@ -386,6 +378,16 @@
                 lambda peer: t2_send.at[pl.ds(a - 1, 2), peer],
                 t2_got.at[pl.ds(a - 1, 2), pl.ds(pl.multiple_of(g * 16, 16), 16), :],
             )
+    arrive(9, 0, u_got)
+    for a in range(4):
+        block = z_in[lanes(a, 4)] + u_got[lanes(a, 4)].astype(F32)
+        middle_t[:, lanes(a)] = block.reshape(128, 128).T
+    for half in range(2):
+        normed = norm0(middle_t[:, lanes(half, 256)]).astype(BF16)
+        home_gate[:, lanes(half, 256)] = jax.nn.sigmoid(
+            jnp.dot(wg_t[1], normed, preferred_element_type=F32)
+        )
+
     for half in range(2):
         arrive(8, half, t2_got.at[pl.ds(2 * half, 2)])
         product = jnp.concatenate(

time: 77.4 us -> 77.8 us (level)
  no operation moved by 1% of the time
where the time goes in v7:
time: 77.8 us; the launch traced here: 77.6 us
  Pallas kernels  76 us (98%)
  local copies, waits for them, and re-layouts  1.67 us (2%)
    pallas_call x1, Pallas kernels, body(): pl.pallas_call(kernel, out_shape=jax.ShapeDtypeStruct((16, 32, 128), F32)...  76 us
    unnamed x1, local copies, waits for them, and re-layouts  1.67 us

profile of v7, /device:TPU:1, one launch (start us, length us, event | category | flops | bytes accessed | tf_op | source)
XLA Modules:
  0.0 77.6 jit_solution(12864069266936517956)
XLA Ops:
  0.0 76.0 %triangles.1 = f32[16,32,128]{2,1,0:T(8,128)} custom-call(f32[16,32,128]{2,1,0:T(8,128)} %z_hbm.1, bf16[128,512]{1,0:T(8,128)(2,1)} %wi0.1, bf16[128,128]{1,0:T(8,128)(2,1)} %wg0.1, bf16[128,128]{1,0:T(8,128)(2,1)} %wf0.1, bf16[128,512]{1,0:T(8,128)(2,1)} %wi1.1, bf16[128,128]{1,0:T(8,128)(2,1)} %wg1.1, bf16[128,128]{1,0:T(8,128)(2,1)} %wf1.1), custom_call_target="tpu_custom_call" | custom-call | tf_op jit(solution)/shard_map/triangles/pallas_call | solution.py:425
  76.0 1.7 %copy.9 = f32[16,32,128]{2,1,0:T(8,128)} copy(f32[16,32,128]{2,1,0:T(8,128)} %triangles.1) | data formatting | bytes 524288

commit v8 on v3

--- a/solution.py
+++ b/solution.py
@@ -90,17 +90,21 @@
                 if dy or dz:
                     yield (y + dy) % 8 * 2 + (zhi + dz) % 2
 
-    def to_owners(phase, chunk, src_of, here):
-        for m in others():
-            send(phase, chunk, src_of(m), here, plane(owner_zlo(m)), m)
-
-        @pl.when(is_owner)
+    def to_owners(phase, chunk, src_of, here, turn_of):
+        for dy in (*FAR_FIRST, 0):
+            peer_y = (y + dy) % 8
+            m = peer_y * 2 + (peer_y // 2 + turn_of) % 2
+            if dy:
+                send(phase, chunk, src_of(m), here, plane(owner_zlo(m)), m)
+        own = jnp.logical_and(is_owner, m == ch)
+
+        @pl.when(own)
         def _():
             keep(phase, chunk, src_of(ch), here)
 
-        @pl.when(jnp.logical_not(is_owner))
+        @pl.when(jnp.logical_not(own))
         def _():
-            send(phase, chunk, src_of(ch), here, plane(owner_zlo(ch)), ch)
+            send(phase, chunk, src_of(m), here, plane(owner_zlo(m)), m)
 
     def both(stage):
         def one(chunk, carry):
@@ -160,6 +164,16 @@
             h_got.at[side, g],
         )
     pl.semaphore_wait(ready, GROUP - 1)
+
+    def first_to_owners(side, turn_of):
+        to_owners(
+            2, side, lambda m: k_send.at[m, side],
+            operands.at[
+                0, side, pl.ds(pl.multiple_of(ch * 32, 32), 32),
+                pl.ds(pl.multiple_of(zlo * 128, 128), 128),
+            ],
+            turn_of,
+        )
 
     for side in range(2):
         arrive(1, side, h_got.at[side])
@@ -179,13 +193,9 @@
                     square.at[q][pl.ds(start, 8, stride=stride), :] = mixed[lanes(q, 8)]
         for q in range(4):
             k_send[4 * q:4 * q + 4, side] = square[q].T.reshape(4, 32, 128).astype(BF16)
-        to_owners(
-            2, side, lambda m: k_send.at[m, side],
-            operands.at[
-                0, side, pl.ds(pl.multiple_of(ch * 32, 32), 32),
-                pl.ds(pl.multiple_of(zlo * 128, 128), 128),
-            ],
-        )
+        first_to_owners(side, 0)
+    for side in range(2):
+        first_to_owners(side, 1)
 
     z_send[...] = z_in[...].astype(BF16)
     spread(
@@ -289,13 +299,15 @@
         arrive(5, chunk, b1_got.at[chunk])
         for side in range(2):
             swap(b1_got.at[chunk, side], lambda c: b2_send.at[chunk, c, side])
-        to_owners(
-            6, chunk, lambda m: b2_send.at[chunk, m],
-            operands.at[
-                1, :, pl.ds(place(zlo, y), 16),
-                pl.ds(pl.multiple_of(chunk * 256 + zhi * 128, 128), 128),
-            ],
-        )
+        for turn_of in range(2):
+            to_owners(
+                6, chunk, lambda m: b2_send.at[chunk, m],
+                operands.at[
+                    1, :, pl.ds(place(zlo, y), 16),
+                    pl.ds(pl.multiple_of(chunk * 256 + zhi * 128, 128), 128),
+                ],
+                turn_of,
+            )
 
     both(second_to_owners)
 

time: 77.4 us -> 78.3 us (1.012)
  Pallas kernels: 75.5 us -> 76.5 us
    pallas_call x1, Pallas kernels: 75.5 us -> 76.5 us  [body(): pl.pallas_call(kernel, out_shape=jax.ShapeDtypeStruct((16, 32, 128), F32)...]
where the time goes in v8:
time: 78.3 us; the launch traced here: 78.2 us
  Pallas kernels  76.5 us (98%)
  local copies, waits for them, and re-layouts  1.67 us (2%)
    pallas_call x1, Pallas kernels, body(): pl.pallas_call(kernel, out_shape=jax.ShapeDtypeStruct((16, 32, 128), F32)...  76.5 us
    unnamed x1, local copies, waits for them, and re-layouts  1.67 us

profile of v8, /device:TPU:1, one launch (start us, length us, event | category | flops | bytes accessed | tf_op | source)
XLA Modules:
  0.0 78.2 jit_solution(6623650554126202447)
XLA Ops:
  0.0 76.5 %triangles.1 = f32[16,32,128]{2,1,0:T(8,128)} custom-call(f32[16,32,128]{2,1,0:T(8,128)} %z_hbm.1, bf16[128,512]{1,0:T(8,128)(2,1)} %wi0.1, bf16[128,128]{1,0:T(8,128)(2,1)} %wg0.1, bf16[128,128]{1,0:T(8,128)(2,1)} %wf0.1, bf16[128,512]{1,0:T(8,128)(2,1)} %wi1.1, bf16[128,128]{1,0:T(8,128)(2,1)} %wg1.1, bf16[128,128]{1,0:T(8,128)(2,1)} %wf1.1), custom_call_target="tpu_custom_call" | custom-call | tf_op jit(solution)/shard_map/triangles/pallas_call | solution.py:435
  76.5 1.7 %copy.9 = f32[16,32,128]{2,1,0:T(8,128)} copy(f32[16,32,128]{2,1,0:T(8,128)} %triangles.1) | data formatting | bytes 524288
